TPU v7x, 32 devices: a whole 2x2x4 slice. The times are simulated.
32 devices in a mesh: slab: 8 (over z, x), grp: 4 (over y, core).
Axes of the slice: x: 2, y: 2, z: 4, core: 2. Of those that a mesh axis runs over, the one named last changes fastest.
Arguments:
- volume: bfloat16 [8, 32, 64, 1024], P('slab', 'grp'), may hold values from -6 to 6
- vis_mask: int32 [8, 32, 64], P('slab', 'grp'), may hold values from 0 to 1, as said below
- enc_gain: bfloat16 [1024], replicated, may hold values from 0.099609375 to 1.8984375
- enc_wqk: bfloat16 [1024, 2048], replicated
- enc_wv: bfloat16 [1024, 1024], replicated, may hold values from -0.1875 to 0.1875
- enc_wo: bfloat16 [1024, 1024], replicated, may hold values from -0.1875 to 0.1875
- final_gain: bfloat16 [1024], replicated, may hold values from 0.099609375 to 1.8984375
- embed_w: bfloat16 [1024, 512], replicated, may hold values from -0.1875 to 0.1875
- mask_token: bfloat16 [512], replicated, may hold values from -4 to 4
- depth_pos: bfloat16 [8, 512], replicated, may hold values from -3 to 3
- row_pos: bfloat16 [32, 512], replicated, may hold values from -3 to 3
- col_pos: bfloat16 [64, 512], replicated, may hold values from -3 to 3
- dec_gain: bfloat16 [512], replicated, may hold values from 0.099609375 to 1.8984375
- dec_wqk: bfloat16 [512, 1024], replicated
- dec_wv: bfloat16 [512, 512], replicated, may hold values from -0.25 to 0.25
- dec_wo: bfloat16 [512, 512], replicated, may hold values from -0.25 to 0.25
Outputs:
- decoded: bfloat16 [8, 32, 64, 512], P('slab', 'grp')
Inputs may be any that keep to these rules, and one draw needn't show every extreme that they name: `vis_mask`: in each block of 8 consecutive depth slices (starting at a multiple of 8) and the 8 plane rows of one grp index, exactly 1024 tokens are visible. The 512 tokens of one depth slice in such a block hold 64 to 192 visible ones, and 192 is reached in every block.
All inputs are finite; a program needn't handle non-finite values.
Results may differ from a plain program's by a relative error of at most 0.0098.
Values may be sent and summed in bfloat16 or wider, within the bound.
A program may use at most 128 MiB of HBM per device.

v0:
```python
import jax
import jax.numpy as jnp
from jax import lax
from jax.sharding import PartitionSpec as P

HEADS = 16
DHEADS = 16
WIN_SLABS = 8
MOST = 192


MASKED = -30000.0


def swapped(block, axis, distance):
    count = lax.axis_size(axis)
    route = []
    for low in range(count):
        high = low | 1 << distance
        if high != low and high < count:
            route += [(low, high), (high, low)]
    return lax.ppermute(block, axis, route)


def layer_norm(values, gain):
    values = values.astype(jnp.float32)
    average = jnp.mean(values, axis=-1, keepdims=True)
    centered = values - average
    variance = jnp.mean(centered * centered, axis=-1, keepdims=True)
    return centered * lax.rsqrt(variance + 1e-05) * gain.astype(jnp.float32)


def softmax_rows(scores):
    row_max = jnp.max(scores, axis=-1, keepdims=True)
    exponent = jnp.exp(scores - row_max)
    return (exponent / jnp.sum(exponent, axis=-1, keepdims=True)).astype(jnp.bfloat16)


def compact(selected, capacity):
    slot_index = jnp.cumsum(selected.astype(jnp.int32)) - 1
    target = jnp.where(selected, slot_index, capacity)
    sources = jnp.arange(selected.shape[0], dtype=jnp.int32)
    row_order = jnp.zeros((capacity,), jnp.int32).at[target].set(sources, mode="drop")
    return (row_order, jnp.sum(selected.astype(jnp.int32)))


def encode(row_data, row_meta, enc_gain, enc_wqk, enc_wv, enc_wo, final_gain, embed_w):
    width = row_data.shape[1]
    head_size = width // HEADS
    normed = layer_norm(row_data, enc_gain).astype(jnp.bfloat16)
    query_key = jnp.dot(normed, enc_wqk, preferred_element_type=jnp.float32).astype(jnp.bfloat16)
    queries = query_key[:, :width]
    key_rows = query_key[:, width:]
    value_rows = jnp.dot(normed, enc_wv, preferred_element_type=jnp.float32).astype(jnp.bfloat16)
    key_bias = jnp.where(row_meta >= 0, 0.0, MASKED).astype(jnp.bfloat16)
    key_rows, value_rows, key_bias = (
        lax.all_gather(key_rows, "grp", axis=0, tiled=True),
        lax.all_gather(value_rows, "grp", axis=0, tiled=True),
        lax.all_gather(key_bias, "grp", axis=0, tiled=True),
    )
    for bit_index in range(WIN_SLABS.bit_length() - 1):
        other_keys, other_values, other_bias = swapped(
            (key_rows, value_rows, key_bias), "slab", bit_index
        )
        key_rows = jnp.concatenate([key_rows, other_keys], axis=0)
        value_rows = jnp.concatenate([value_rows, other_values], axis=0)
        key_bias = jnp.concatenate([key_bias, other_bias], axis=0)
    bias_row = key_bias.astype(jnp.float32)[None, :]
    score_scale = head_size ** (-0.5)

    def head_context(head_index):
        offset = head_index * head_size
        query_part = lax.dynamic_slice_in_dim(queries, offset, head_size, 1)
        key_part = lax.dynamic_slice_in_dim(key_rows, offset, head_size, 1)
        value_part = lax.dynamic_slice_in_dim(value_rows, offset, head_size, 1)
        scores = lax.dot_general(
            query_part, key_part, (((1,), (1,)), ((), ())), preferred_element_type=jnp.float32
        )
        scores = scores * score_scale + bias_row
        return jnp.dot(softmax_rows(scores), value_part, preferred_element_type=jnp.float32).astype(
            jnp.bfloat16
        )

    context = lax.map(head_context, jnp.arange(HEADS, dtype=jnp.int32))
    context = jnp.transpose(context, (1, 0, 2)).reshape(row_data.shape[0], width)
    mixed = row_data.astype(jnp.float32) + jnp.dot(
        context, enc_wo, preferred_element_type=jnp.float32
    )
    encoded = layer_norm(mixed, final_gain).astype(jnp.bfloat16)
    return jnp.dot(encoded, embed_w, preferred_element_type=jnp.float32).astype(jnp.bfloat16)


def decode_rows(block, dec_gain, dec_wqk, dec_wv, dec_wo):
    depth, single, count, width = block.shape
    head_size = width // DHEADS
    block = block.reshape(depth, count, width)
    normed = layer_norm(block, dec_gain).astype(jnp.bfloat16).reshape(depth * count, width)
    query_key = jnp.dot(normed, dec_wqk, preferred_element_type=jnp.float32).astype(jnp.bfloat16)
    value_rows = jnp.dot(normed, dec_wv, preferred_element_type=jnp.float32).astype(jnp.bfloat16)
    queries = query_key[:, :width].reshape(depth, count, DHEADS, head_size)
    key_rows = query_key[:, width:].reshape(depth, count, DHEADS, head_size)
    value_rows = value_rows.reshape(depth, count, DHEADS, head_size)
    scores = jnp.einsum(
        "zphd,yphd->phzy", queries, key_rows, preferred_element_type=jnp.float32
    ) * head_size ** (-0.5)
    probs = softmax_rows(scores)
    context = jnp.einsum("phzy,yphd->zphd", probs, value_rows, preferred_element_type=jnp.float32)
    context = context.astype(jnp.bfloat16).reshape(depth * count, width)
    mixed = block.reshape(depth * count, width).astype(jnp.float32) + jnp.dot(
        context, dec_wo, preferred_element_type=jnp.float32
    )
    return mixed.astype(jnp.bfloat16).reshape(depth, single, count, width)


def per_device(
    volume,
    vis_mask,
    enc_gain,
    enc_wqk,
    enc_wv,
    enc_wo,
    final_gain,
    embed_w,
    mask_token,
    depth_pos,
    row_pos,
    col_pos,
    dec_gain,
    dec_wqk,
    dec_wv,
    dec_wo,
):
    plane_rows = volume.shape[1]
    plane_cols = volume.shape[2]
    width = volume.shape[3]
    tokens_dev = plane_rows * plane_cols
    flat_volume = volume.reshape(tokens_dev, width)
    visible = vis_mask.reshape(tokens_dev) == 1
    row_order, row_count = compact(visible, MOST)
    slots = jnp.arange(MOST, dtype=jnp.int32)
    row_data = flat_volume[row_order]
    row_meta = jnp.where(slots < row_count, row_order, -1)
    embedded = encode(row_data, row_meta, enc_gain, enc_wqk, enc_wv, enc_wo, final_gain, embed_w)
    dec_width = embedded.shape[1]
    target = jnp.where(row_meta >= 0, row_meta % tokens_dev, tokens_dev)
    tokens_in = jnp.broadcast_to(mask_token[None, :], (tokens_dev, dec_width))
    tokens_in = tokens_in.at[target].set(embedded, mode="drop")
    depth_index = lax.axis_index("slab")
    group_index = lax.axis_index("grp")
    depth_row = lax.dynamic_slice_in_dim(depth_pos, depth_index, 1, 0).astype(jnp.float32)
    plane_pos = lax.dynamic_slice_in_dim(row_pos, group_index * plane_rows, plane_rows, 0).astype(
        jnp.float32
    )
    streams = (
        tokens_in.astype(jnp.float32).reshape(plane_rows, plane_cols, dec_width)
        + depth_row[None, :, :]
    )
    streams = streams + plane_pos[:, None, :]
    streams = streams + col_pos.astype(jnp.float32)[None, :, :]
    slab_count = lax.axis_size("slab")
    streams = streams.astype(jnp.bfloat16).reshape(
        1, slab_count, tokens_dev // slab_count, dec_width
    )
    columns = decode_rows(
        lax.all_to_all(streams, "slab", split_axis=1, concat_axis=0, tiled=True),
        dec_gain,
        dec_wqk,
        dec_wv,
        dec_wo,
    )
    decoded = lax.all_to_all(columns, "slab", split_axis=0, concat_axis=1, tiled=True)
    return decoded.reshape(1, plane_rows, plane_cols, dec_width)


def solution(mesh):
    placed = (
        P("slab", "grp", None, None),
        P("slab", "grp", None),
        P(),
        P(),
        P(),
        P(),
        P(),
        P(),
        P(),
        P(),
        P(),
        P(),
        P(),
        P(),
        P(),
        P(),
    )
    return jax.shard_map(
        per_device,
        mesh=mesh,
        in_specs=placed,
        out_specs=P("slab", "grp", None, None),
        check_vma=False,
    )
```

profile of v0, /device:TPU:0, one launch (start us, length us, event | category | flops | bytes accessed | tf_op | source)
XLA Modules:
  0.0 939.4 jit_solution(17585300551457566525)
XLA Ops:
  22.2 18.4 %all-gather.5.cloned.1.call-done = bf16[768,1024]{1,0:T(8,128)(2,1)} async-done(((bf16[192,1024]{1,0:T(8,128)(2,1)}), bf16[768,1024]{1,0:T(8,128)(2,1)}) %all-gather.5.cloned.1.call-update) | async-done | bytes 1572880 | tf_op jit(solution)/shard_map/all_gather | solution.py:58
  42.0 19.8 %all-gather.3.cloned.1.call-done = bf16[768,1024]{1,0:T(8,128)(2,1)} async-done(((bf16[192,1024]{1,0:T(8,128)(2,1)}), bf16[768,1024]{1,0:T(8,128)(2,1)}) %all-gather.3.cloned.1.call-update) | async-done | bytes 1572880 | tf_op jit(solution)/shard_map/all_gather | solution.py:57
  63.3 14.8 %collective-permute-done.6 = bf16[768,1024]{1,0:T(8,128)(2,1)} collective-permute-done((bf16[768,1024]{1,0:T(8,128)(2,1)}, bf16[768,1024]{1,0:T(8,128)(2,1)}, u32[]{:S(2)}, u32[]{:S(2)}) %collective-permute-start.6) | collective-permute-done | bytes 1572896 | tf_op jit(solution)/shard_map/ppermute | solution.py:22
  81.9 29.2 %collective-permute-done = bf16[768,1024]{1,0:T(8,128)(2,1)S(1)} collective-permute-done((bf16[768,1024]{1,0:T(8,128)(2,1)}, bf16[768,1024]{1,0:T(8,128)(2,1)S(1)}, u32[]{:S(2)}, u32[]{:S(2)}) %collective-permute-start) | collective-permute-done | bytes 1572896 | tf_op jit(solution)/shard_map/ppermute | solution.py:22
  114.7 36.8 %collective-permute-done.7 = bf16[1536,1024]{1,0:T(8,128)(2,1)} collective-permute-done((bf16[1536,1024]{1,0:T(8,128)(2,1)S(1)}, bf16[1536,1024]{1,0:T(8,128)(2,1)}, u32[]{:S(2)}, u32[]{:S(2)}) %collective-permute-start.7) | collective-permute-done | bytes 3145760 | tf_op jit(solution)/shard_map/ppermute | solution.py:22
  151.5 5.8 pad_maximum_fusion.3
  159.8 118.7 %collective-permute-done.1 = bf16[1536,1024]{1,0:T(8,128)(2,1)} collective-permute-done((bf16[1536,1024]{1,0:T(8,128)(2,1)}, bf16[1536,1024]{1,0:T(8,128)(2,1)}, u32[]{:S(2)}, u32[]{:S(2)}) %collective-permute-start.1) | collective-permute-done | bytes 3145760 | tf_op jit(solution)/shard_map/ppermute | solution.py:22
  278.5 10.7 %pad_maximum_fusion.2 = bf16[3072,1024]{1,0:T(8,128)(2,1)} fusion(bf16[1536,1024]{1,0:T(8,128)(2,1)} %collective-permute-done.1, bf16[768,1024]{1,0:T(8,128)(2,1)S(1)} %collective-permute-done, bf16[768,1024]{1,0:T(8,128)(2,1)S(1)} %copy-done.2), kind=kLoop, calls=%fused_computation.20 | loop fusion | flops 18874368 | bytes 12582912 | tf_op jit(solution)/shard_map/concatenate | solution.py:65
  291.3 6.2 all-reduce
  303.9 181.5 %collective-permute-done.4 = bf16[1536]{0:T(1024)(128)(2,1)S(1)} collective-permute-done((bf16[1536]{0:T(1024)(128)(2,1)S(1)}, bf16[1536]{0:T(1024)(128)(2,1)S(1)}, u32[]{:S(2)}, u32[]{:S(2)}) %collective-permute-start.4) | collective-permute-done | bytes 3104 | tf_op jit(solution)/shard_map/ppermute | solution.py:22
  485.4 3.4 collective-permute-start.5
  490.2 206.0 %collective-permute-done.5 = bf16[3072]{0:T(1024)(128)(2,1)S(1)} collective-permute-done((bf16[3072]{0:T(1024)(128)(2,1)S(1)}, bf16[3072]{0:T(1024)(128)(2,1)S(1)}, u32[]{:S(2)}, u32[]{:S(2)}) %collective-permute-start.5) | collective-permute-done | bytes 6176 | tf_op jit(solution)/shard_map/ppermute | solution.py:22
  696.3 11.9 %pad_maximum_fusion.1 = bf16[6144,1024]{1,0:T(8,128)(2,1)} fusion(bf16[3072,1024]{1,0:T(8,128)(2,1)} %collective-permute-done.8, bf16[1536,1024]{1,0:T(8,128)(2,1)} %collective-permute-done.7, bf16[768,1024]{1,0:T(8,128)(2,1)} %collective-permute-done.6, bf16[768,1024]{1,0:T(8,128)(2,1)} %all-gather.5.cloned.1.call-done), kind=kLoop, calls=%fused_computation.19 | loop fusion | flops 50331648 | bytes 25165824 | tf_op jit(solution)/shard_map/concatenate | solution.py:66
  708.2 10.6 %pad_maximum_fusion = bf16[6144,1024]{1,0:T(8,128)(2,1)} fusion(bf16[3072,1024]{1,0:T(8,128)(2,1)} %collective-permute-done.2, bf16[1536,1024]{1,0:T(8,128)(2,1)} %collective-permute-done.1, bf16[768,1024]{1,0:T(8,128)(2,1)S(1)} %copy-done.5, bf16[768,1024]{1,0:T(8,128)(2,1)S(1)} %copy-done.3), kind=kLoop, calls=%fused_computation.18 | loop fusion | flops 50331648 | bytes 25165824 | tf_op jit(solution)/shard_map/concatenate | solution.py:65
  718.8 124.7 %while.10 = (s32[]{:T(128)}, bf16[16,192,64]{1,2,0:T(8,128)(2,1)S(1)}, s32[16]{0:T(128)S(1)}, bf16[192,1024]{1,0:T(8,128)(2,1)S(1)}, bf16[6144,1024]{1,0:T(8,128...) while((s32[]{:T(128)}, ...), condition=%wide.region_9.10_spmd, body=%wide.region_6.9_spmd.sunk | while | flops 311438976 | bytes 17414060 | solution.py:84
  847.8 5.5 all-to-all-start
  853.3 10.3 %all-to-all-done = bf16[1,8,64,512]{3,2,0,1:T(8,128)(2,1)S(1)} async-done(((bf16[1,8,64,512]{3,2,0,1:T(8,128)(2,1)}), bf16[1,8,64,512]{3,2,0,1:T(8,128)(2,1)S(1)}, u32[]{:S(2)}, u32[]{:S(2)}) %all-to-all-start) | async-done | bytes 524320 | tf_op jit(solution)/shard_map/all_to_all | solution.py:165
  871.9 5.5 copy.32
  881.8 5.5 copy.33
  892.4 5.6 copy.34
  898.0 7.1 fusion.53
  905.2 4.7 convert_bitcast_fusion
  909.9 4.7 copy.36
  918.0 13.8 %all_to_all.21 = bf16[8,1,64,512]{3,2,1,0:T(8,128)(2,1)S(1)} all-to-all(bf16[8,1,64,512]{3,2,1,0:T(8,128)(2,1)S(1)} %bitcast.75), channel_id=1, replica_groups=mesh['slab'=8,'grp'=4] {'slab'}, dimensions={0} | all-to-all | bytes 1048576 | tf_op jit(solution)/shard_map/all_to_all | solution.py:171
  (177 shorter events, 177.9 us)
Async XLA Ops:
  6.5 837.0 %copy-start = (bf16[1024,1024]{1,0:T(8,128)(2,1)S(1)}, bf16[1024,1024]{1,0:T(8,128)(2,1)}, u32[]{:S(2)}) copy-start(bf16[1024,1024]{1,0:T(8,128)(2,1)} %param.23) | copy-start | bytes 6291460
  6.5 8.5 copy-start.9
  6.5 34.0 %all-gather.5.cloned.1.call-start = ((), (), s32[]{:S(2)}) async-start(), calls=%async_computation.3 | async-start | bytes 1966080 | tf_op jit(solution)/shard_map/all_gather | solution.py:58
  18.1 43.8 %all-gather.3.cloned.1.call-start = ((), (), s32[]{:S(2)}) async-start(), calls=%async_computation.2 | async-start | bytes 1966080 | tf_op jit(solution)/shard_map/all_gather | solution.py:57
  40.6 37.5 %collective-permute-start.6 = (bf16[768,1024]{1,0:T(8,128)(2,1)}, bf16[768,1024]{1,0:T(8,128)(2,1)}, u32[]{:S(2)}, u32[]{:S(2)}) collective-permute-start(bf16[768,1024]{1,0:T(8,128)(2,1)} %all-gather.5.cloned.1.call-done), channel_id=1, source_target_pairs={{0,4},{4,0},{8,12},{12,8},{16,20},{20,16},{24,28},{28,24},{1,5},{5... | collective-permute-start | bytes 4718600 | tf_op jit(solution)/shard_map/ppermute | solution.py:22
  61.8 49.2 %copy-start.2 = (bf16[768,1024]{1,0:T(8,128)(2,1)S(1)}, bf16[768,1024]{1,0:T(8,128)(2,1)}, u32[]{:S(2)}) copy-start(bf16[768,1024]{1,0:T(8,128)(2,1)} %all-gather.3.cloned.1.call-done) | copy-start | bytes 4718596
  61.8 49.2 %collective-permute-start = (bf16[768,1024]{1,0:T(8,128)(2,1)}, bf16[768,1024]{1,0:T(8,128)(2,1)S(1)}, u32[]{:S(2)}, u32[]{:S(2)}) collective-permute-start(bf16[768,1024]{1,0:T(8,128)(2,1)} %all-gather.3.cloned.1.call-done), channel_id=1, source_target_pairs={{0,4},{4,0},{8,12},{12,8},{16,20},{20,16},{24,28},{28,24},{1,5},{5... | collective-permute-start | bytes 4718600 | tf_op jit(solution)/shard_map/ppermute | solution.py:22
  80.3 71.2 %copy-start.1 = (bf16[768,1024]{1,0:T(8,128)(2,1)S(1)}, bf16[768,1024]{1,0:T(8,128)(2,1)}, u32[]{:S(2)}) copy-start(bf16[768,1024]{1,0:T(8,128)(2,1)} %all-gather.5.cloned.1.call-done) | copy-start | bytes 4718596
  80.3 71.2 %collective-permute-start.7 = (bf16[1536,1024]{1,0:T(8,128)(2,1)S(1)}, bf16[1536,1024]{1,0:T(8,128)(2,1)}, u32[]{:S(2)}, u32[]{:S(2)}) collective-permute-start(bf16[1536,1024]{1,0:T(8,128)(2,1)S(1)} %pad_maximum_fusion.5), channel_id=1, source_target_pairs={{0,8},{8,0},{4,12},{12,4},{16,24},{24,16},{20,28},{28,20},{1,9},{9... | collective-permute-start | bytes 9437192 | tf_op jit(solution)/shard_map/ppermute | solution.py:22
  111.0 167.5 %copy-start.4 = (bf16[768,1024]{1,0:T(8,128)(2,1)}, bf16[768,1024]{1,0:T(8,128)(2,1)S(1)}, u32[]{:S(2)}) copy-start(bf16[768,1024]{1,0:T(8,128)(2,1)S(1)} %collective-permute-done) | copy-start | bytes 4718596
  113.2 165.3 %collective-permute-start.1 = (bf16[1536,1024]{1,0:T(8,128)(2,1)}, bf16[1536,1024]{1,0:T(8,128)(2,1)}, u32[]{:S(2)}, u32[]{:S(2)}) collective-permute-start(bf16[1536,1024]{1,0:T(8,128)(2,1)} %pad_maximum_fusion.4), channel_id=1, source_target_pairs={{0,8},{8,0},{4,12},{12,4},{16,24},{24,16},{20,28},{28,20},{1,9},{9... | collective-permute-start | bytes 9437192 | tf_op jit(solution)/shard_map/ppermute | solution.py:22
  157.3 131.9 %copy-start.13 = (u32[32]{0:T(128)S(1)}, u32[32]{0:T(128)}, u32[]{:S(2)}) copy-start(u32[32]{0:T(128)} %constant.89) | copy-start | bytes 388
  157.3 332.2 %copy-start.10 = (bf16[1024]{0:T(1024)(128)(2,1)S(1)}, bf16[1024]{0:T(1024)(128)(2,1)}, u32[]{:S(2)}) copy-start(bf16[1024]{0:T(1024)(128)(2,1)} %param.24) | copy-start | bytes 6148
  157.4 332.2 %copy-start.8 = (bf16[64,512]{1,0:T(8,128)(2,1)S(1)}, bf16[64,512]{1,0:T(8,128)(2,1)}, u32[]{:S(2)}) copy-start(bf16[64,512]{1,0:T(8,128)(2,1)} %param.29) | copy-start | bytes 196612
  157.4 538.9 %collective-permute-start.8 = (bf16[3072,1024]{1,0:T(8,128)(2,1)}, bf16[3072,1024]{1,0:T(8,128)(2,1)}, u32[]{:S(2)}, u32[]{:S(2)}) collective-permute-start(bf16[3072,1024]{1,0:T(8,128)(2,1)} %pad_maximum_fusion.3), channel_id=1, source_target_pairs={{0,16},{16,0},{4,20},{20,4},{8,24},{24,8},{12,28},{28,12},{1,17},{... | collective-permute-start | bytes 18874376 | tf_op jit(solution)/shard_map/ppermute | solution.py:22
  289.2 419.0 %collective-permute-start.2 = (bf16[3072,1024]{1,0:T(8,128)(2,1)}, bf16[3072,1024]{1,0:T(8,128)(2,1)}, u32[]{:S(2)}, u32[]{:S(2)}) collective-permute-start(bf16[3072,1024]{1,0:T(8,128)(2,1)} %pad_maximum_fusion.2), channel_id=1, source_target_pairs={{0,16},{16,0},{4,20},{20,4},{8,24},{24,8},{12,28},{28,12},{1,17},{... | collective-permute-start | bytes 18874376 | tf_op jit(solution)/shard_map/ppermute | solution.py:22
  297.5 3.6 collective-permute-start.3
  301.2 184.2 %collective-permute-start.4 = (bf16[1536]{0:T(1024)(128)(2,1)S(1)}, bf16[1536]{0:T(1024)(128)(2,1)S(1)}, u32[]{:S(2)}, u32[]{:S(2)}) collective-permute-start(bf16[1536]{0:T(1024)(128)(2,1)S(1)} %pad_maximum_fusion.7), channel_id=1, source_target_pairs={{0,8},{8,0},{4,12},{12,4},{16,24},{24,16},{20,28},{28,20},{1,9},{9... | collective-permute-start | bytes 9224 | tf_op jit(solution)/shard_map/ppermute | solution.py:22
  485.4 210.8 %collective-permute-start.5 = (bf16[3072]{0:T(1024)(128)(2,1)S(1)}, bf16[3072]{0:T(1024)(128)(2,1)S(1)}, u32[]{:S(2)}, u32[]{:S(2)}) collective-permute-start(bf16[3072]{0:T(1024)(128)(2,1)S(1)} %pad_maximum_fusion.6), channel_id=1, source_target_pairs={{0,16},{16,0},{4,20},{20,4},{8,24},{24,8},{12,28},{28,12},{1,17},{... | collective-permute-start | bytes 18440 | tf_op jit(solution)/shard_map/ppermute | solution.py:22
  696.3 11.9 %copy-start.3 = (bf16[768,1024]{1,0:T(8,128)(2,1)S(1)}, bf16[768,1024]{1,0:T(8,128)(2,1)}, u32[]{:S(2)}) copy-start(bf16[768,1024]{1,0:T(8,128)(2,1)} %all-gather.3.cloned.1.call-done) | copy-start | bytes 4718596
  696.3 11.9 %copy-start.5 = (bf16[768,1024]{1,0:T(8,128)(2,1)S(1)}, bf16[768,1024]{1,0:T(8,128)(2,1)}, u32[]{:S(2)}) copy-start(bf16[768,1024]{1,0:T(8,128)(2,1)} %copy-done.4) | copy-start | bytes 4718596
  844.2 2.6 copy-start.7
  844.5 8.8 copy-start.12
  847.8 15.8 %all-to-all-start = ((bf16[1,8,64,512]{3,2,0,1:T(8,128)(2,1)}), bf16[1,8,64,512]{3,2,0,1:T(8,128)(2,1)S(1)}, u32[]{:S(2)}, u32[]{:S(2)}) async-start(bf16[1,8,64,512]{3,2,0,1:T(8,128)(2,1)} %fusion.27), calls=%async_computation | async-start | bytes 1048576 | tf_op jit(solution)/shard_map/all_to_all | solution.py:165
  (2 other events, 2.9 us)
Sparse Core Ops, SparseCore 0:
  18.2 22.3 all-gather.4
  42.1 19.6 all-gather.2
where the time goes:
time: 942 us; the launch traced here: 939 us
  waiting for transfers between devices  638 us (68%)
  matrix products  117 us (12%)
  other arithmetic  63.9 us (7%)
  local copies, waits for them, and re-layouts  55.4 us (6%)
  starting transfers between devices  20.9 us (2%)
  blocking collectives  20 us (2%)
  between operations  14.4 us (2%)
  loops' own time  10.5 us (1%)
    ppermute x9, waiting for transfers between devices, swapped(): return lax.ppermute(block, axis, route)  589 us
    dot_general x16, matrix products, head_context(): jnp.dot(softmax_rows(scores), value_part, preferred_element_type=jnp.floa...  50.6 us
    dot_general x16, matrix products, head_context(): lax.dot_general(query_part, key_part, (((1,), (1,)), ((), ())), preferred...  41.1 us
    concatenate x3, other arithmetic, encode(): key_rows = jnp.concatenate([key_rows, other_keys], axis=0)  23.5 us
    concatenate x3, other arithmetic, encode(): value_rows = jnp.concatenate([value_rows, other_values], axis=0)  19.9 us
    all_gather x1, waiting for transfers between devices, encode(): lax.all_gather(key_rows, 'grp', axis=0, tiled=True)  19.8 us
  transfers between devices with their start and end apart: 12, of which 10 were waited for; matrix products, arithmetic and copies ran while one was open for 4% of the time, Pallas kernels for 0%

commit v1 on v0

v1 whole, which is shorter than its diff:
```python
import functools

import jax
import jax.numpy as jnp
from jax import lax
from jax.experimental import pallas as pl
from jax.experimental.pallas import tpu as pltpu
from jax.sharding import Mesh, PartitionSpec as P

HEADS = 16
DHEADS = 16
WIN_SLABS = 8
MOST = 192
HALF = MOST // 2
COUNT_ROWS = 16
KV_ROWS = MOST + COUNT_ROWS
SEND_ROWS = KV_ROWS + HALF
QUAD = 4
LOG2E = 1.4426950408889634
F32 = jnp.float32
BF16 = jnp.bfloat16


def dot(a, b):
    return lax.dot_general(a, b, (((1,), (0,)), ((), ())), preferred_element_type=F32)


def dot_nt(a, b):
    return lax.dot_general(a, b, (((1,), (1,)), ((), ())), preferred_element_type=F32)


def norm(values, gain):
    average = jnp.mean(values, axis=-1, keepdims=True)
    centered = values - average
    variance = jnp.mean(centered * centered, axis=-1, keepdims=True)
    return centered * lax.rsqrt(variance + 1e-05) * gain.astype(F32)


def iota(shape, dim):
    return lax.broadcasted_iota(jnp.int32, shape, dim)


def project_kernel(mask, volume, gain, wq, wk, wv, sent, rows, normed):
    tokens = volume.shape[0]

    @pl.when(pl.program_id(0) == 0)
    def _():
        seen = mask[...] == 1
        seen_rows = jnp.broadcast_to(jnp.where(seen, 1.0, 0.0), (16, tokens)).astype(BF16)
        upper = jnp.where(iota((tokens, tokens), 0) <= iota((tokens, tokens), 1), 1.0, 0.0)
        rank = dot(seen_rows, upper.astype(BF16))[0:1, :].astype(jnp.int32) - 1
        rank = jnp.where(seen, rank, -1)
        pick = jnp.where(iota((MOST, tokens), 0) == rank, 1.0, 0.0).astype(BF16)
        row_data = dot(pick, volume[...])
        rows[...] = row_data.astype(BF16)
        normed[...] = norm(row_data, gain[...]).astype(BF16)

    count = jnp.sum(jnp.where(mask[...] == 1, 1.0, 0.0), axis=1, keepdims=True)
    x = normed[...]
    size = wq.shape[1] // QUAD
    q = dot(x, wq[...]) * (size ** (-0.5) * LOG2E)
    k = dot(x, wk[...])
    v = dot(x, wv[...])
    for i in range(QUAD):
        part = slice(i * size, (i + 1) * size)
        sent[i, 0:MOST, :] = jnp.concatenate([k[:, part], v[:, part]], axis=1).astype(BF16)
        sent[i, MOST:KV_ROWS, :] = jnp.broadcast_to(count, (COUNT_ROWS, 2 * size)).astype(BF16)
        sent[i, KV_ROWS:SEND_ROWS, :] = jnp.concatenate(
            [q[0:HALF, part], q[HALF:MOST, part]], axis=1
        ).astype(BF16)


def project(mask, volume, gain, wqk, wv):
    tokens, width = volume.shape
    steps = HEADS // QUAD
    cols = width // steps
    lanes = 2 * (width // HEADS)
    return pl.pallas_call(
        project_kernel,
        grid=(steps,),
        in_specs=[
            pl.BlockSpec((1, tokens), lambda j: (0, 0)),
            pl.BlockSpec((tokens, width), lambda j: (0, 0)),
            pl.BlockSpec((1, width), lambda j: (0, 0)),
            pl.BlockSpec((width, cols), lambda j: (0, j)),
            pl.BlockSpec((width, cols), lambda j: (0, j + steps)),
            pl.BlockSpec((width, cols), lambda j: (0, j)),
        ],
        out_specs=[
            pl.BlockSpec((QUAD, SEND_ROWS, lanes), lambda j: (j, 0, 0)),
            pl.BlockSpec((MOST, width), lambda j: (0, 0)),
        ],
        out_shape=[
            jax.ShapeDtypeStruct((HEADS, SEND_ROWS, lanes), BF16),
            jax.ShapeDtypeStruct((MOST, width), BF16),
        ],
        scratch_shapes=[pltpu.VMEM((MOST, width), BF16)],
        compiler_params=pltpu.CompilerParams(vmem_limit_bytes=40 << 20),
        name="project",
    )(mask, volume, gain, wqk, wqk, wv)


TILE = 256


def attend_kernel(counts, mine, other, out, packed, queries, keys, values, results):
    blocks = mine.shape[0]
    lanes = mine.shape[2]
    size = lanes // 2
    total = keys.shape[0]
    half = total // 2
    zero = jnp.zeros((MOST, size), F32)
    offset = 0
    starts = []
    for i in range(2 * blocks):
        source = mine if i < blocks else other
        packed[pl.ds(offset, MOST), :] = source[i % blocks, 0:MOST, :].astype(F32)
        if i < blocks:
            starts.append(offset)
        offset = offset + counts[i]
    for i in range(0, total, TILE):
        both = packed[i : i + TILE, :]
        keys[i : i + TILE, :] = both.astype(BF16)
        values[i : i + TILE, :] = jnp.where(iota((TILE, lanes), 1) < size, 1.0, both).astype(BF16)
    for i in range(blocks):
        q = mine[i, KV_ROWS:SEND_ROWS, :].astype(F32)
        q = jnp.concatenate([q[:, :size], q[:, size:]], axis=0)
        packed[pl.ds(starts[i], MOST), :] = jnp.concatenate([q, zero], axis=1)
    for i in range(0, half, TILE):
        queries[i : i + TILE, :] = packed[i : i + TILE, :].astype(BF16)
    results[half:, :] = jnp.zeros((results.shape[0] - half, lanes), F32)

    def step(t, carry):
        at = pl.multiple_of(t * TILE, TILE)
        scores = dot_nt(queries[pl.ds(at, TILE), :], keys[...])
        top = jnp.max(scores, axis=-1, keepdims=True)
        weight = jnp.exp2(scores - top).astype(BF16)
        mixed = dot(weight, values[...])
        results[pl.ds(at, TILE), :] = mixed / pltpu.roll(mixed, size, 1)
        return carry

    lax.fori_loop(0, half // TILE, step, 0)
    for i in range(blocks):
        block = results[pl.ds(starts[i], MOST), :][:, size:]
        out[i, :, :] = jnp.concatenate([block[0:HALF], block[HALF:MOST]], axis=1).astype(BF16)


def attend(counts, mine, other, total):
    blocks, _, lanes = mine.shape
    whole = pl.BlockSpec(memory_space=pltpu.VMEM)
    return pl.pallas_call(
        attend_kernel,
        in_specs=[pl.BlockSpec(memory_space=pltpu.SMEM), whole, whole],
        out_specs=whole,
        out_shape=jax.ShapeDtypeStruct((blocks, HALF, lanes), BF16),
        scratch_shapes=[
            pltpu.VMEM((total + MOST, lanes), F32),
            pltpu.VMEM((total // 2, lanes), BF16),
            pltpu.VMEM((total, lanes), BF16),
            pltpu.VMEM((total, lanes), BF16),
            pltpu.VMEM((total // 2 + MOST, lanes), F32),
        ],
        compiler_params=pltpu.CompilerParams(vmem_limit_bytes=48 << 20),
        name="attend",
    )(counts, mine, other)


def merge_kernel(
    plane_rows, mask, rows, context, wo, gain, embed, mask_token, depth_pos, row_pos, col_pos, out
):
    tokens = out.shape[0]
    plane_cols = tokens // plane_rows
    heads, _, lanes = context.shape
    size = lanes // 2
    tiles = []
    for j in range(0, heads, 2):
        a, b = context[j], context[j + 1]
        tiles.append(
            jnp.concatenate(
                [
                    jnp.concatenate([a[:, :size], b[:, :size]], axis=1),
                    jnp.concatenate([a[:, size:], b[:, size:]], axis=1),
                ],
                axis=0,
            )
        )
    mixed = rows[...].astype(F32) + dot(jnp.concatenate(tiles, axis=1), wo[...])
    encoded = norm(mixed, gain[...]).astype(BF16)
    embedded = dot(encoded, embed[...]).astype(BF16)

    seen = jnp.broadcast_to(jnp.where(mask[...] == 1, 1.0, 0.0), (16, tokens)).astype(BF16)
    down, across = iota((tokens, tokens), 0), iota((tokens, tokens), 1)
    rank = dot_nt(jnp.where(across <= down, 1.0, 0.0).astype(BF16), seen)[:, 0:1]
    shown = dot_nt(jnp.where(across == down, 1.0, 0.0).astype(BF16), seen)[:, 0:1] > 0.5
    rank = jnp.where(shown, rank.astype(jnp.int32) - 1, -1)
    place = jnp.where(iota((tokens, MOST), 1) == rank, 1.0, 0.0).astype(BF16)
    stream = dot(place, embedded)
    stream = jnp.where(shown, stream, mask_token[...].astype(F32))

    depth = lax.axis_index("win") * lax.axis_size("slab") + lax.axis_index("slab")
    grp = lax.axis_index("y") * lax.axis_size("half") + lax.axis_index("half")
    depths = depth_pos[...].astype(F32)
    chosen = jnp.where(iota(depths.shape, 0) == depth, depths, 0.0)
    stream = stream + jnp.sum(chosen, axis=0, keepdims=True)
    row_count, col_count = row_pos.shape[0], col_pos.shape[0]
    row = iota((tokens, row_count), 0) // plane_cols + grp * plane_rows
    row_hot = jnp.where(iota((tokens, row_count), 1) == row, 1.0, 0.0).astype(BF16)
    stream = stream + dot(row_hot, row_pos[...])
    col = iota((tokens, col_count), 0) % plane_cols
    col_hot = jnp.where(iota((tokens, col_count), 1) == col, 1.0, 0.0).astype(BF16)
    stream = stream + dot(col_hot, col_pos[...])
    out[...] = stream.astype(BF16)


def merge(plane_rows, mask, rows, context, wo, gain, embed, mask_token, *positions):
    tokens = mask.shape[1]
    whole = pl.BlockSpec(memory_space=pltpu.VMEM)
    return pl.pallas_call(
        functools.partial(merge_kernel, plane_rows),
        in_specs=[whole] * 10,
        out_specs=whole,
        out_shape=jax.ShapeDtypeStruct((tokens, embed.shape[1]), BF16),
        compiler_params=pltpu.CompilerParams(vmem_limit_bytes=40 << 20),
        name="merge",
    )(mask, rows, context, wo, gain, embed, mask_token, *positions)


def decode_kernel(depth, block, gain, wqk, wv, wo, out, queries, keys, values, context):
    tokens, width = block.shape
    spots = tokens // depth
    size = width // DHEADS
    x = block[...].astype(F32)
    normed = norm(x, gain[...]).astype(BF16)
    queries[...] = dot(normed, wqk[:, :width]).astype(BF16).astype(F32)
    keys[...] = dot(normed, wqk[:, width:]).astype(BF16).astype(F32)
    values[...] = dot(normed, wv[...]).astype(BF16).astype(F32)
    lanes = 128
    gather = jnp.where(iota((width, lanes), 0) // size == iota((width, lanes), 1), 1.0, 0.0)
    gather = gather.astype(BF16)
    spread = jnp.where(iota((lanes, width), 1) // size == iota((lanes, width), 0), 1.0, 0.0)
    spread = spread.astype(BF16)

    def step(z, carry):
        at = pl.multiple_of(z * spots, spots)
        query = queries[pl.ds(at, spots), :]
        product = keys[...].reshape(depth, spots, width) * query[None]
        product = product.reshape(tokens, width)
        high = product.astype(BF16)
        low = (product - high.astype(F32)).astype(BF16)
        scores = (dot(high, gather) + dot(low, gather)) * size ** (-0.5)
        scores = scores.reshape(depth, spots, lanes)
        exponent = jnp.exp(scores - jnp.max(scores, axis=0, keepdims=True))
        probs = exponent / jnp.sum(exponent, axis=0, keepdims=True)
        wide = dot(probs.reshape(tokens, lanes).astype(BF16), spread)
        context[pl.ds(at, spots), :] = jnp.sum(
            (wide * values[...]).reshape(depth, spots, width), axis=0
        )
        return carry

    lax.fori_loop(0, depth, step, 0)
    out[...] = (x + dot(context[...].astype(BF16), wo[...])).astype(BF16)


def decode(depth, block, gain, wqk, wv, wo):
    whole = pl.BlockSpec(memory_space=pltpu.VMEM)
    return pl.pallas_call(
        functools.partial(decode_kernel, depth),
        in_specs=[whole] * 5,
        out_specs=whole,
        out_shape=jax.ShapeDtypeStruct(block.shape, BF16),
        scratch_shapes=[pltpu.VMEM(block.shape, F32)] * 4,
        compiler_params=pltpu.CompilerParams(vmem_limit_bytes=40 << 20),
        name="decode",
    )(block, gain, wqk, wv, wo)


def per_device(
    volume,
    vis_mask,
    enc_gain,
    enc_wqk,
    enc_wv,
    enc_wo,
    final_gain,
    embed_w,
    mask_token,
    depth_pos,
    row_pos,
    col_pos,
    dec_gain,
    dec_wqk,
    dec_wv,
    dec_wo,
):
    _, plane_rows, plane_cols, width = volume.shape
    tokens = plane_rows * plane_cols
    mask = vis_mask.reshape(1, tokens)
    sent, rows = project(
        mask, volume.reshape(tokens, width), enc_gain.reshape(1, width), enc_wqk, enc_wv
    )
    mine = lax.all_to_all(sent, ("slab", "y"), split_axis=0, concat_axis=0, tiled=True)
    other = lax.ppermute(mine[:, :KV_ROWS, :], "half", [(0, 1), (1, 0)])
    counts = jnp.concatenate([mine[:, MOST, 0], other[:, MOST, 0]]).astype(jnp.int32)
    window_tokens = WIN_SLABS * tokens * lax.axis_size("y") * lax.axis_size("half")
    context = attend(counts, mine, other, window_tokens // 4)
    context = lax.all_to_all(context, ("slab", "y"), split_axis=0, concat_axis=0, tiled=True)
    streams = merge(
        plane_rows,
        mask,
        rows,
        context,
        enc_wo,
        final_gain.reshape(1, width),
        embed_w,
        mask_token.reshape(1, -1),
        depth_pos,
        row_pos,
        col_pos,
    )
    slabs = ("win", "slab")
    depth = depth_pos.shape[0]
    columns = lax.all_to_all(streams, slabs, split_axis=0, concat_axis=0, tiled=True)
    columns = decode(depth, columns, dec_gain.reshape(1, -1), dec_wqk, dec_wv, dec_wo)
    decoded = lax.all_to_all(columns, slabs, split_axis=0, concat_axis=0, tiled=True)
    return decoded.reshape(1, plane_rows, plane_cols, -1)


def solution(mesh):
    slabs, groups = mesh.devices.shape
    split = Mesh(
        mesh.devices.reshape(slabs // WIN_SLABS, WIN_SLABS, groups // 2, 2),
        ("win", "slab", "y", "half"),
    )
    placed = (
        P(("win", "slab"), ("y", "half"), None, None),
        P(("win", "slab"), ("y", "half"), None),
    ) + (P(),) * 14
    return jax.shard_map(
        per_device,
        mesh=split,
        in_specs=placed,
        out_specs=P(("win", "slab"), ("y", "half"), None, None),
        check_vma=False,
    )
```

time: 942 us -> 139 us (0.15)
  waiting for transfers between devices: 638 us -> 26.6 us
  matrix products: 117 us -> 0 us
  other arithmetic: 63.9 us -> 0.08 us
  local copies, waits for them, and re-layouts: 55.4 us -> 16.9 us
  blocking collectives: 20 us -> 56.9 us
  Pallas kernels: 0 us -> 30.3 us
  between operations: 14.4 us -> 0.09 us
  starting transfers between devices: 20.9 us -> 7.13 us
  loops' own time: 10.5 us -> 0 us
    ppermute x9 -> x1, waiting for transfers between devices: 589 us -> 2.16 us  [per_device(): other = lax.ppermute(mine[:, :KV_ROWS, :], 'half', [(0, 1), (1, 0)])]
    dot_general x40 -> x0, matrix products: 109 us -> none  [the longest x16 50.6 us: head_context(): jnp.dot(softmax_rows(scores), value_part, preferred_element_type=jnp.floa...]
    concatenate x8 -> x0, other arithmetic: 43.4 us -> none  [the longest x3 23.5 us: encode(): key_rows = jnp.concatenate([key_rows, other_keys], axis=0)]
    all_to_all x1 -> x2, blocking collectives: 13.8 us -> 56.9 us  [the longest x1 39.4 us: per_device(): lax.all_to_all(sent, ('slab', 'y'), split_axis=0, concat_axis=0, tiled=True)]
    all_gather x2 -> x0, waiting for transfers between devices: 38.1 us -> none  [the longest x1 19.8 us: encode(): lax.all_gather(key_rows, 'grp', axis=0, tiled=True)]
    pallas_call x0 -> x4, Pallas kernels: none -> 30.3 us  [the longest x1 14 us: attend(): pl.pallas_call(attend_kernel, in_specs=[pl.BlockSpec(memory_space=pltpu.S...]
    reshape x7 -> x5, local copies, waits for them, and re-layouts: 24.8 us -> 4.09 us  [the longest x1 1.27 us: per_device(): mask_token.reshape(1, -1)]
    reduce_sum x22 -> x0, other arithmetic: 15.5 us -> none  [the longest x16 12.9 us: softmax_rows(): jnp.sum(exponent, axis=-1, keepdims=True)]
  transfers between devices with their start and end apart: 12 -> 3, of which waited for: 10 -> 3; matrix products, arithmetic and copies ran while one was open for 4% -> 2% of each run, Pallas kernels for 0% -> 0%
where the time goes in v1:
time: 139 us; the launch traced here: 138 us
  blocking collectives  56.9 us (41%)
  Pallas kernels  30.3 us (22%)
  waiting for transfers between devices  26.6 us (19%)
  local copies, waits for them, and re-layouts  16.9 us (12%)
  starting transfers between devices  7.13 us (5%)
    all_to_all x1, blocking collectives, per_device(): lax.all_to_all(sent, ('slab', 'y'), split_axis=0, concat_axis=0, tiled=True)  39.4 us
    all_to_all x1, blocking collectives, per_device(): lax.all_to_all(columns, slabs, split_axis=0, concat_axis=0, tiled=True)  17.6 us
    pallas_call x1, Pallas kernels, attend(): pl.pallas_call(attend_kernel, in_specs=[pl.BlockSpec(memory_space=pltpu.S...  14 us
    all_to_all x1, waiting for transfers between devices, per_device(): lax.all_to_all(streams, slabs, split_axis=0, concat_axis=0, tiled=True)  13.2 us
    unnamed x29, local copies, waits for them, and re-layouts  12.4 us
    all_to_all x1, waiting for transfers between devices, per_device(): lax.all_to_all(context, ('slab', 'y'), split_axis=0, concat_axis=0, tiled...  11.2 us
    pallas_call x1, Pallas kernels, decode(): pl.pallas_call(functools.partial(decode_kernel, depth), in_specs=[whole]...  9.59 us
    pallas_call x1, Pallas kernels, project(): pl.pallas_call(project_kernel, grid=(steps,), in_specs=[pl.BlockSpec((1,...  4 us
  transfers between devices with their start and end apart: 3, of which 3 were waited for; matrix products, arithmetic and copies ran while one was open for 2% of the time, Pallas kernels for 0%

profile of v1, /device:TPU:0, one launch (start us, length us, event | category | flops | bytes accessed | tf_op | source)
XLA Modules:
  0.0 138.0 jit_solution(14057711431562232602)
XLA Ops:
  0.0 0.8 reshape.26.mask
  1.5 2.2 %copy-done = bf16[1024,2048]{1,0:T(8,128)(2,1)S(1)} copy-done((bf16[1024,2048]{1,0:T(8,128)(2,1)S(1)}, bf16[1024,2048]{1,0:T(8,128)(2,1)}, u32[]{:S(2)}) %copy-start) | copy-done | bytes 4194328
  3.6 1.6 %copy-done.2 = bf16[1024,1024]{1,0:T(8,128)(2,1)S(1)} copy-done((bf16[1024,1024]{1,0:T(8,128)(2,1)S(1)}, bf16[1024,1024]{1,0:T(8,128)(2,1)}, u32[]{:S(2)}) %copy-start.2) | copy-done | bytes 2097176
  5.2 1.2 copy-done.3
  6.5 4.0 %project.1 = (bf16[16,304,128]{2,1,0:T(8,128)(2,1)S(1)}, bf16[192,1024]{1,0:T(8,128)(2,1)S(1)}) custom-call(s32[1,512]{1,0:T(1,128)S(1)} %reshape.26.mask, bf16[512,1024]{1,0:T(8,128)(2,1)S(1)} %bitcast.7, bf16[1,1024]{1,0:T(2,128)(2,1)S(1)} %reshape.28.gain, bf16[1024,2048]{1,0:T(8,128)(2,1)S(1)} %copy-done, bf16[1024,2048]{1,0:T(8,128)(2,1)S(1)} %copy-done, ...), custom_call_target="tpu_custom_call" | custom-call | tf_op jit(solution)/shard_map/project/pallas_call | solution.py:78
  10.5 39.4 %all_to_all.30.mine = bf16[16,304,128]{2,1,0:T(8,128)(2,1)S(1)} all-to-all(bf16[16,304,128]{2,1,0:T(8,128)(2,1)S(1)} %get-tuple-element.8), channel_id=1, replica_groups=mesh['win'=1,'slab'=8,'y'=2,'half'=2] {'slab','y'}, dimensions={0} | all-to-all | bytes 2490368 | tf_op jit(solution)/shard_map/all_to_all | solution.py:301
  50.2 2.2 %collective-permute-done.other = bf16[16,208,128]{2,1,0:T(8,128)(2,1)S(1)} collective-permute-done((bf16[16,208,128]{2,1,0:T(8,128)(2,1)S(1)}, bf16[16,208,128]{2,1,0:T(8,128)(2,1)S(1)}, u32[]{:S(2)}, u32[]{:S(2)}) %collective-permute-start) | collective-permute-done | bytes 852000 | tf_op jit(solution)/shard_map/ppermute | solution.py:302
  52.6 14.0 %attend.1 = bf16[16,96,128]{2,1,0:T(8,128)(2,1)} custom-call(s32[32]{0:T(128)S(1)} %maximum_convert_fusion.counts, bf16[16,304,128]{2,1,0:T(8,128)(2,1)S(1)} %all_to_all.30.mine, bf16[16,208,128]{2,1,0:T(8,128)(2,1)S(1)} %collective-permute-done.other), custom_call_target="tpu_custom_call" | custom-call | tf_op jit(solution)/shard_map/attend/pallas_call | solution.py:151
  66.6 3.6 %all-to-all-start.1 = ((bf16[16,96,128]{2,1,0:T(8,128)(2,1)}), bf16[16,96,128]{2,1,0:T(8,128)(2,1)S(1)}, u32[]{:S(2)}, u32[]{:S(2)}) async-start(bf16[16,96,128]{2,1,0:T(8,128)(2,1)} %attend.1), calls=%async_computation.1 | async-start | bytes 786432 | tf_op jit(solution)/shard_map/all_to_all | solution.py:306
  70.2 0.7 reshape.29.gain
  70.9 1.3 reshape.30.mask_token
  72.2 11.2 %all-to-all-done.1.context = bf16[16,96,128]{2,1,0:T(8,128)(2,1)S(1)} async-done(((bf16[16,96,128]{2,1,0:T(8,128)(2,1)}), bf16[16,96,128]{2,1,0:T(8,128)(2,1)S(1)}, u32[]{:S(2)}, u32[]{:S(2)}) %all-to-all-start.1) | async-done | bytes 393248 | tf_op jit(solution)/shard_map/all_to_all | solution.py:306
  83.3 1.0 copy-done.9
  84.3 0.8 copy-done.10
  85.2 0.8 copy-done.11
  86.6 2.7 %merge.1 = bf16[512,512]{1,0:T(8,128)(2,1)} custom-call(s32[1,512]{1,0:T(1,128)S(1)} %reshape.26.mask, bf16[192,1024]{1,0:T(8,128)(2,1)S(1)} %copy-done.9, bf16[16,96,128]{2,1,0:T(8,128)(2,1)S(1)} %all-to-all-done.1.context, bf16[1024,1024]{1,0:T(8,128)(2,1)S(1)} %copy-done.1, bf16[1,1024]{1,0:T(2,128)(2,1)S(1)} %reshape.29.gain, ...), custom_call_target="tpu_custom_call" | custom-call | tf_op jit(solution)/shard_map/merge/pallas_call | solution.py:218
  89.3 3.5 %all-to-all-start.2 = ((bf16[8,64,512]{2,1,0:T(8,128)(2,1)}), bf16[8,64,512]{2,1,0:T(8,128)(2,1)S(1)}, u32[]{:S(2)}, u32[]{:S(2)}) async-start(bf16[8,64,512]{2,1,0:T(8,128)(2,1)} %bitcast.1), calls=%async_computation.2 | async-start | bytes 1048576 | tf_op jit(solution)/shard_map/all_to_all | solution.py:322
  93.5 13.2 %all-to-all-done.2 = bf16[8,64,512]{2,1,0:T(8,128)(2,1)S(1)} async-done(((bf16[8,64,512]{2,1,0:T(8,128)(2,1)}), bf16[8,64,512]{2,1,0:T(8,128)(2,1)S(1)}, u32[]{:S(2)}, u32[]{:S(2)}) %all-to-all-start.2) | async-done | bytes 524320 | tf_op jit(solution)/shard_map/all_to_all | solution.py:322
  106.8 1.2 copy-done.5
  108.0 1.0 copy-done.6
  109.0 1.0 copy-done.7
  110.1 9.6 %decode.1 = bf16[512,512]{1,0:T(8,128)(2,1)S(1)} custom-call(bf16[512,512]{1,0:T(8,128)(2,1)S(1)} %bitcast.5, bf16[1,512]{1,0:T(2,128)(2,1)S(1)} %reshape.31.gain, bf16[512,1024]{1,0:T(8,128)(2,1)S(1)} %copy-done.5, bf16[512,512]{1,0:T(8,128)(2,1)S(1)} %copy-done.6, bf16[512,512]{1,0:T(8,128)(2,1)S(1)} %copy-done.7), custom_call_target="tpu_custom_call" | custom-call | tf_op jit(solution)/shard_map/decode/pallas_call | solution.py:266
  119.7 17.6 %all_to_all.31 = bf16[8,64,512]{2,1,0:T(8,128)(2,1)S(1)} all-to-all(bf16[8,64,512]{2,1,0:T(8,128)(2,1)S(1)} %bitcast.6), channel_id=1, replica_groups=mesh['win'=1,'slab'=8,'y'=2,'half'=2] {'win','slab'}, dimensions={0} | all-to-all | bytes 1048576 | tf_op jit(solution)/shard_map/all_to_all | solution.py:324
  137.2 0.8 copy.18
  (26 shorter events, 2.7 us)
Async XLA Ops:
  1.4 2.2 %copy-start = (bf16[1024,2048]{1,0:T(8,128)(2,1)S(1)}, bf16[1024,2048]{1,0:T(8,128)(2,1)}, u32[]{:S(2)}) copy-start(bf16[1024,2048]{1,0:T(8,128)(2,1)} %wk.1) | copy-start | bytes 12582916
  3.6 1.6 %copy-start.2 = (bf16[1024,1024]{1,0:T(8,128)(2,1)S(1)}, bf16[1024,1024]{1,0:T(8,128)(2,1)}, u32[]{:S(2)}) copy-start(bf16[1024,1024]{1,0:T(8,128)(2,1)} %wv.2) | copy-start | bytes 6291460
  5.2 1.2 copy-start.3
  10.5 39.4 %copy-start.8 = (bf16[192,1024]{1,0:T(8,128)(2,1)}, bf16[192,1024]{1,0:T(8,128)(2,1)S(1)}, u32[]{:S(2)}) copy-start(bf16[192,1024]{1,0:T(8,128)(2,1)S(1)} %get-tuple-element.7.rows) | copy-start | bytes 1179652
  49.8 33.5 %copy-start.1 = (bf16[1024,1024]{1,0:T(8,128)(2,1)S(1)}, bf16[1024,1024]{1,0:T(8,128)(2,1)}, u32[]{:S(2)}) copy-start(bf16[1024,1024]{1,0:T(8,128)(2,1)} %wo.2) | copy-start | bytes 6291460
  49.8 33.5 %copy-start.4 = (bf16[1024,512]{1,0:T(8,128)(2,1)S(1)}, bf16[1024,512]{1,0:T(8,128)(2,1)}, u32[]{:S(2)}) copy-start(bf16[1024,512]{1,0:T(8,128)(2,1)} %embed.1) | copy-start | bytes 3145732
  49.8 33.5 %copy-start.12 = (bf16[8,512]{1,0:T(8,128)(2,1)S(1)}, bf16[8,512]{1,0:T(8,128)(2,1)}, u32[]{:S(2)}) copy-start(bf16[8,512]{1,0:T(8,128)(2,1)} %depth_pos.1) | copy-start | bytes 24580
  49.9 2.4 %collective-permute-start = (bf16[16,208,128]{2,1,0:T(8,128)(2,1)S(1)}, bf16[16,208,128]{2,1,0:T(8,128)(2,1)S(1)}, u32[]{:S(2)}, u32[]{:S(2)}) collective-permute-start(bf16[16,208,128]{2,1,0:T(8,128)(2,1)S(1)} %slice.13), channel_id=1, source_target_pairs={{0,1},{1,0},{2,3},{3,2},{4,5},{5,4},{6,7},{7,6},{8,9},{9,8},{10,11... | collective-permute-start | bytes 2555912 | tf_op jit(solution)/shard_map/ppermute | solution.py:302
  66.6 16.7 %all-to-all-start.1 = ((bf16[16,96,128]{2,1,0:T(8,128)(2,1)}), bf16[16,96,128]{2,1,0:T(8,128)(2,1)S(1)}, u32[]{:S(2)}, u32[]{:S(2)}) async-start(bf16[16,96,128]{2,1,0:T(8,128)(2,1)} %attend.1), calls=%async_computation.1 | async-start | bytes 786432 | tf_op jit(solution)/shard_map/all_to_all | solution.py:306
  83.3 1.0 copy-start.9
  84.3 0.8 copy-start.10
  85.2 0.8 copy-start.11
  85.9 0.7 copy-start.13
  89.3 17.4 %all-to-all-start.2 = ((bf16[8,64,512]{2,1,0:T(8,128)(2,1)}), bf16[8,64,512]{2,1,0:T(8,128)(2,1)S(1)}, u32[]{:S(2)}, u32[]{:S(2)}) async-start(bf16[8,64,512]{2,1,0:T(8,128)(2,1)} %bitcast.1), calls=%async_computation.2 | async-start | bytes 1048576 | tf_op jit(solution)/shard_map/all_to_all | solution.py:322
  106.8 1.2 copy-start.5
  108.0 1.0 copy-start.6
  109.0 1.0 copy-start.7

commit v2 on v1

--- a/solution.py
+++ b/solution.py
@@ -19,6 +19,7 @@
 LOG2E = 1.4426950408889634
 F32 = jnp.float32
 BF16 = jnp.bfloat16
+MESH = pl.DeviceIdType.MESH
 
 
 def dot(a, b):
@@ -165,16 +166,118 @@
     )(counts, mine, other)
 
 
-def merge_kernel(
-    plane_rows, mask, rows, context, wo, gain, embed, mask_token, depth_pos, row_pos, col_pos, out
+def finish_kernel(
+    plane_rows,
+    context,
+    mask,
+    rows,
+    gain,
+    mask_token,
+    depth_pos,
+    row_pos,
+    col_pos,
+    dec_gain,
+    wo_hbm,
+    embed_hbm,
+    wqk_hbm,
+    wv_hbm,
+    dec_wo_hbm,
+    out,
+    wo,
+    embed,
+    wqk,
+    wv,
+    dec_wo,
+    landed,
+    streams,
+    columns,
+    queries,
+    keys,
+    values,
+    decoded,
+    load_sem,
+    head_send,
+    head_recv,
+    part_send,
+    part_recv,
+    back_send,
+    back_recv,
 ):
-    tokens = out.shape[0]
+    slab, y = lax.axis_index("slab"), lax.axis_index("y")
+    y_count, slab_count = lax.axis_size("y"), lax.axis_size("slab")
+    heads, _, lanes = context.shape
+    depth, spots, dec_width = out.shape
+    tokens = depth * spots
     plane_cols = tokens // plane_rows
-    heads, _, lanes = context.shape
+    head = slab * y_count + y
+    level = lax.axis_index("win") * slab_count + slab
     size = lanes // 2
+
+    loads = []
+    for i, (source, target) in enumerate(
+        ((wo_hbm, wo), (embed_hbm, embed), (wqk_hbm, wqk), (wv_hbm, wv), (dec_wo_hbm, dec_wo))
+    ):
+        load = pltpu.make_async_copy(source, target, load_sem.at[i])
+        load.start()
+        loads.append(load)
+
+    def head_device(i):
+        peer = lax.rem(head + i, heads)
+        return peer, {"slab": peer // y_count, "y": lax.rem(peer, y_count)}
+
+    def level_device(i):
+        peer = lax.rem(level + i, depth)
+        return peer, {"win": peer // slab_count, "slab": lax.rem(peer, slab_count)}
+
+    barrier = pltpu.get_barrier_semaphore()
+    for i in range(1, heads):
+        _, place = head_device(i)
+        pl.semaphore_signal(barrier, inc=1, device_id=place, device_id_type=MESH)
+    for i in range(1, depth):
+        _, place = level_device(i)
+        pl.semaphore_signal(barrier, inc=1, device_id=place, device_id_type=MESH)
+    pl.semaphore_wait(barrier, heads + depth - 2)
+
+    head_copies = []
+    for i in range(1, heads):
+        peer, place = head_device(i)
+        copy = pltpu.make_async_remote_copy(
+            src_ref=context.at[peer],
+            dst_ref=landed.at[head],
+            send_sem=head_send.at[i],
+            recv_sem=head_recv.at[i],
+            device_id=place,
+            device_id_type=MESH,
+        )
+        copy.start()
+        head_copies.append(copy)
+    landed[head] = context[head]
+
+    seen = jnp.broadcast_to(jnp.where(mask[...] == 1, 1.0, 0.0), (16, tokens)).astype(BF16)
+    down, across = iota((tokens, tokens), 0), iota((tokens, tokens), 1)
+    rank = dot_nt(jnp.where(across <= down, 1.0, 0.0).astype(BF16), seen)[:, 0:1]
+    shown = dot_nt(jnp.where(across == down, 1.0, 0.0).astype(BF16), seen)[:, 0:1] > 0.5
+    rank = jnp.where(shown, rank.astype(jnp.int32) - 1, -1)
+    place = jnp.where(iota((tokens, MOST), 1) == rank, 1.0, 0.0).astype(BF16)
+    grp = y * lax.axis_size("half") + lax.axis_index("half")
+    depths = depth_pos[...].astype(F32)
+    chosen = jnp.where(iota(depths.shape, 0) == level, depths, 0.0)
+    chosen = jnp.sum(chosen, axis=0, keepdims=True)
+    row_count, col_count = row_pos.shape[0], col_pos.shape[0]
+    row = iota((tokens, row_count), 0) // plane_cols + grp * plane_rows
+    row_hot = jnp.where(iota((tokens, row_count), 1) == row, 1.0, 0.0).astype(BF16)
+    row_part = dot(row_hot, row_pos[...])
+    col = iota((tokens, col_count), 0) % plane_cols
+    col_hot = jnp.where(iota((tokens, col_count), 1) == col, 1.0, 0.0).astype(BF16)
+    col_part = dot(col_hot, col_pos[...])
+
+    loads[0].wait()
+    loads[1].wait()
+    for copy in head_copies:
+        copy.wait()
     tiles = []
     for j in range(0, heads, 2):
-        a, b = context[j], context[j + 1]
+        a, b = landed[j], landed[j + 1]
         tiles.append(
             jnp.concatenate(
                 [
@@ -187,91 +290,125 @@
     mixed = rows[...].astype(F32) + dot(jnp.concatenate(tiles, axis=1), wo[...])
     encoded = norm(mixed, gain[...]).astype(BF16)
     embedded = dot(encoded, embed[...]).astype(BF16)
-
-    seen = jnp.broadcast_to(jnp.where(mask[...] == 1, 1.0, 0.0), (16, tokens)).astype(BF16)
-    down, across = iota((tokens, tokens), 0), iota((tokens, tokens), 1)
-    rank = dot_nt(jnp.where(across <= down, 1.0, 0.0).astype(BF16), seen)[:, 0:1]
-    shown = dot_nt(jnp.where(across == down, 1.0, 0.0).astype(BF16), seen)[:, 0:1] > 0.5
-    rank = jnp.where(shown, rank.astype(jnp.int32) - 1, -1)
-    place = jnp.where(iota((tokens, MOST), 1) == rank, 1.0, 0.0).astype(BF16)
     stream = dot(place, embedded)
     stream = jnp.where(shown, stream, mask_token[...].astype(F32))
-
-    depth = lax.axis_index("win") * lax.axis_size("slab") + lax.axis_index("slab")
-    grp = lax.axis_index("y") * lax.axis_size("half") + lax.axis_index("half")
-    depths = depth_pos[...].astype(F32)
-    chosen = jnp.where(iota(depths.shape, 0) == depth, depths, 0.0)
-    stream = stream + jnp.sum(chosen, axis=0, keepdims=True)
-    row_count, col_count = row_pos.shape[0], col_pos.shape[0]
-    row = iota((tokens, row_count), 0) // plane_cols + grp * plane_rows
-    row_hot = jnp.where(iota((tokens, row_count), 1) == row, 1.0, 0.0).astype(BF16)
-    stream = stream + dot(row_hot, row_pos[...])
-    col = iota((tokens, col_count), 0) % plane_cols
-    col_hot = jnp.where(iota((tokens, col_count), 1) == col, 1.0, 0.0).astype(BF16)
-    stream = stream + dot(col_hot, col_pos[...])
-    out[...] = stream.astype(BF16)
-
-
-def merge(plane_rows, mask, rows, context, wo, gain, embed, mask_token, *positions):
-    tokens = mask.shape[1]
-    whole = pl.BlockSpec(memory_space=pltpu.VMEM)
-    return pl.pallas_call(
-        functools.partial(merge_kernel, plane_rows),
-        in_specs=[whole] * 10,
-        out_specs=whole,
-        out_shape=jax.ShapeDtypeStruct((tokens, embed.shape[1]), BF16),
-        compiler_params=pltpu.CompilerParams(vmem_limit_bytes=40 << 20),
-        name="merge",
-    )(mask, rows, context, wo, gain, embed, mask_token, *positions)
-
-
-def decode_kernel(depth, block, gain, wqk, wv, wo, out, queries, keys, values, context):
-    tokens, width = block.shape
-    spots = tokens // depth
-    size = width // DHEADS
-    x = block[...].astype(F32)
-    normed = norm(x, gain[...]).astype(BF16)
-    queries[...] = dot(normed, wqk[:, :width]).astype(BF16).astype(F32)
-    keys[...] = dot(normed, wqk[:, width:]).astype(BF16).astype(F32)
-    values[...] = dot(normed, wv[...]).astype(BF16).astype(F32)
-    lanes = 128
-    gather = jnp.where(iota((width, lanes), 0) // size == iota((width, lanes), 1), 1.0, 0.0)
-    gather = gather.astype(BF16)
-    spread = jnp.where(iota((lanes, width), 1) // size == iota((lanes, width), 0), 1.0, 0.0)
-    spread = spread.astype(BF16)
-
-    def step(z, carry):
-        at = pl.multiple_of(z * spots, spots)
-        query = queries[pl.ds(at, spots), :]
-        product = keys[...].reshape(depth, spots, width) * query[None]
-        product = product.reshape(tokens, width)
+    stream = ((stream + chosen) + row_part) + col_part
+    streams[...] = stream.reshape(depth, spots, dec_width).astype(BF16)
+
+    def part_copy(i):
+        peer, where = level_device(i)
+        return pltpu.make_async_remote_copy(
+            src_ref=streams.at[peer],
+            dst_ref=columns.at[level],
+            send_sem=part_send.at[i],
+            recv_sem=part_recv.at[i],
+            device_id=where,
+            device_id_type=MESH,
+        )
+
+    def back_copy(i):
+        peer, where = level_device(i)
+        return pltpu.make_async_remote_copy(
+            src_ref=decoded.at[peer],
+            dst_ref=out.at[level],
+            send_sem=back_send.at[i],
+            recv_sem=back_recv.at[i],
+            device_id=where,
+            device_id_type=MESH,
+        )
+
+    def start_part(i, carry):
+        part_copy(i).start()
+        return carry
+
+    lax.fori_loop(1, depth, start_part, 0)
+    columns[level] = streams[level]
+    for load in loads[2:]:
+        load.wait()
+
+    def wait_part(i, carry):
+        part_copy(i).wait()
+        return carry
+
+    lax.fori_loop(1, depth, wait_part, 0)
+    x = columns[...].astype(F32).reshape(tokens, dec_width)
+    normed = norm(x, dec_gain[...]).astype(BF16)
+    shape = (depth, spots, dec_width)
+    queries[...] = dot(normed, wqk[:, :dec_width]).astype(BF16).astype(F32).reshape(shape)
+    keys[...] = dot(normed, wqk[:, dec_width:]).astype(BF16).astype(F32).reshape(shape)
+    values[...] = dot(normed, wv[...]).astype(BF16).astype(F32).reshape(shape)
+    dec_size = dec_width // DHEADS
+    wide = 128
+    gather = jnp.where(
+        iota((dec_width, wide), 0) // dec_size == iota((dec_width, wide), 1), 1.0, 0.0
+    ).astype(BF16)
+    spread = jnp.where(
+        iota((wide, dec_width), 1) // dec_size == iota((wide, dec_width), 0), 1.0, 0.0
+    ).astype(BF16)
+
+    def decode(z):
+        product = (keys[...] * queries[z][None]).reshape(tokens, dec_width)
         high = product.astype(BF16)
         low = (product - high.astype(F32)).astype(BF16)
-        scores = (dot(high, gather) + dot(low, gather)) * size ** (-0.5)
-        scores = scores.reshape(depth, spots, lanes)
+        scores = (dot(high, gather) + dot(low, gather)) * dec_size ** (-0.5)
+        scores = scores.reshape(depth, spots, wide)
         exponent = jnp.exp(scores - jnp.max(scores, axis=0, keepdims=True))
         probs = exponent / jnp.sum(exponent, axis=0, keepdims=True)
-        wide = dot(probs.reshape(tokens, lanes).astype(BF16), spread)
-        context[pl.ds(at, spots), :] = jnp.sum(
-            (wide * values[...]).reshape(depth, spots, width), axis=0
-        )
+        probs = dot(probs.reshape(tokens, wide).astype(BF16), spread).reshape(shape)
+        result = jnp.sum(probs * values[...], axis=0).astype(BF16)
+        return (columns[z].astype(F32) + dot(result, dec_wo[...])).astype(BF16)
+
+    def step(i, carry):
+        z = lax.rem(level + i, depth)
+        decoded[z] = decode(z)
+        back_copy(i).start()
         return carry
 
-    lax.fori_loop(0, depth, step, 0)
-    out[...] = (x + dot(context[...].astype(BF16), wo[...])).astype(BF16)
-
-
-def decode(depth, block, gain, wqk, wv, wo):
+    lax.fori_loop(1, depth, step, 0)
+    out[level] = decode(level)
+
+    def wait_back(i, carry):
+        back_copy(i).wait()
+        return carry
+
+    lax.fori_loop(1, depth, wait_back, 0)
+
+
+def finish(plane_rows, depth, context, mask, rows, *others):
+    tokens = mask.shape[1]
+    weights = others[-5:]
+    dec_width = weights[1].shape[1]
+    heads = context.shape[0]
     whole = pl.BlockSpec(memory_space=pltpu.VMEM)
+    shape = (depth, tokens // depth, dec_width)
+    dma = pltpu.SemaphoreType.DMA
     return pl.pallas_call(
-        functools.partial(decode_kernel, depth),
-        in_specs=[whole] * 5,
+        functools.partial(finish_kernel, plane_rows),
+        in_specs=[whole] * 9 + [pl.BlockSpec(memory_space=pl.ANY)] * 5,
         out_specs=whole,
-        out_shape=jax.ShapeDtypeStruct(block.shape, BF16),
-        scratch_shapes=[pltpu.VMEM(block.shape, F32)] * 4,
-        compiler_params=pltpu.CompilerParams(vmem_limit_bytes=40 << 20),
-        name="decode",
-    )(block, gain, wqk, wv, wo)
+        out_shape=jax.ShapeDtypeStruct(shape, BF16),
+        scratch_shapes=[pltpu.VMEM(w.shape, BF16) for w in weights]
+        + [
+            pltpu.VMEM(context.shape, BF16),
+            pltpu.VMEM(shape, BF16),
+            pltpu.VMEM(shape, BF16),
+            pltpu.VMEM(shape, F32),
+            pltpu.VMEM(shape, F32),
+            pltpu.VMEM(shape, F32),
+            pltpu.VMEM(shape, BF16),
+            dma((5,)),
+            dma((heads,)),
+            dma((heads,)),
+            dma((depth,)),
+            dma((depth,)),
+            dma((depth,)),
+            dma((depth,)),
+        ],
+        compiler_params=pltpu.CompilerParams(
+            vmem_limit_bytes=48 << 20, collective_id=1, has_side_effects=True
+        ),
+        name="finish",
+    )(context, mask, rows, *others)
 
 
 def per_device(
@@ -303,25 +440,24 @@
     counts = jnp.concatenate([mine[:, MOST, 0], other[:, MOST, 0]]).astype(jnp.int32)
     window_tokens = WIN_SLABS * tokens * lax.axis_size("y") * lax.axis_size("half")
     context = attend(counts, mine, other, window_tokens // 4)
-    context = lax.all_to_all(context, ("slab", "y"), split_axis=0, concat_axis=0, tiled=True)
-    streams = merge(
+    decoded = finish(
         plane_rows,
+        depth_pos.shape[0],
+        context,
         mask,
         rows,
-        context,
-        enc_wo,
         final_gain.reshape(1, width),
-        embed_w,
         mask_token.reshape(1, -1),
         depth_pos,
         row_pos,
         col_pos,
+        dec_gain.reshape(1, -1),
+        enc_wo,
+        embed_w,
+        dec_wqk,
+        dec_wv,
+        dec_wo,
     )
-    slabs = ("win", "slab")
-    depth = depth_pos.shape[0]
-    columns = lax.all_to_all(streams, slabs, split_axis=0, concat_axis=0, tiled=True)
-    columns = decode(depth, columns, dec_gain.reshape(1, -1), dec_wqk, dec_wv, dec_wo)
-    decoded = lax.all_to_all(columns, slabs, split_axis=0, concat_axis=0, tiled=True)
     return decoded.reshape(1, plane_rows, plane_cols, -1)
 
 

time: 139 us -> 108 us (0.78)
  Pallas kernels: 30.3 us -> 57.1 us
  waiting for transfers between devices: 26.6 us -> 2.09 us
  blocking collectives: 56.9 us -> 39.5 us
  local copies, waits for them, and re-layouts: 16.9 us -> 7.78 us
  starting transfers between devices: 7.13 us -> 0.07 us
    pallas_call x2 -> x1, Pallas kernels: 12.3 us -> 39.8 us  [finish(): pl.pallas_call(functools.partial(finish_kernel, plane_rows), in_specs=[wh...]
    all_to_all x2 -> x0, waiting for transfers between devices: 24.4 us -> none  [the longest x1 13.2 us: per_device(): lax.all_to_all(streams, slabs, split_axis=0, concat_axis=0, tiled=True)]
    all_to_all x1 -> x0, blocking collectives: 17.6 us -> none  [per_device(): lax.all_to_all(columns, slabs, split_axis=0, concat_axis=0, tiled=True)]
    all_to_all x2 -> x0, starting transfers between devices: 7.06 us -> none  [the longest x1 3.55 us: per_device(): lax.all_to_all(context, ('slab', 'y'), split_axis=0, concat_axis=0, tiled...]
    unnamed x29 -> x27, local copies, waits for them, and re-layouts: 12.4 us -> 5.85 us
  transfers between devices with their start and end apart: 3 -> 1, of which waited for: 3 -> 1; matrix products, arithmetic and copies ran while one was open for 2% -> 0% of each run, Pallas kernels for 0% -> 0%
where the time goes in v2:
time: 108 us; the launch traced here: 107 us
  Pallas kernels  57.1 us (53%)
  blocking collectives  39.5 us (37%)
  local copies, waits for them, and re-layouts  7.78 us (7%)
  waiting for transfers between devices  2.09 us (2%)
    pallas_call x1, Pallas kernels, finish(): pl.pallas_call(functools.partial(finish_kernel, plane_rows), in_specs=[wh...  39.8 us
    all_to_all x1, blocking collectives, per_device(): lax.all_to_all(sent, ('slab', 'y'), split_axis=0, concat_axis=0, tiled=True)  39.5 us
    pallas_call x1, Pallas kernels, attend(): pl.pallas_call(attend_kernel, in_specs=[pl.BlockSpec(memory_space=pltpu.S...  13.3 us
    unnamed x27, local copies, waits for them, and re-layouts  5.85 us
    pallas_call x1, Pallas kernels, project(): pl.pallas_call(project_kernel, grid=(steps,), in_specs=[pl.BlockSpec((1,...  4 us
  transfers between devices with their start and end apart: 1, of which 1 were waited for; matrix products, arithmetic and copies ran while one was open for 0% of the time, Pallas kernels for 0%

profile of v2, /device:TPU:0, one launch (start us, length us, event | category | flops | bytes accessed | tf_op | source)
XLA Modules:
  0.0 106.8 jit_solution(15401218112021873413)
XLA Ops:
  0.0 0.8 reshape.21.mask
  0.8 0.7 reshape.23.gain
  1.5 2.2 %copy-done = bf16[1024,2048]{1,0:T(8,128)(2,1)S(1)} copy-done((bf16[1024,2048]{1,0:T(8,128)(2,1)S(1)}, bf16[1024,2048]{1,0:T(8,128)(2,1)}, u32[]{:S(2)}) %copy-start) | copy-done | bytes 4194328
  3.6 1.6 %copy-done.1 = bf16[1024,1024]{1,0:T(8,128)(2,1)S(1)} copy-done((bf16[1024,1024]{1,0:T(8,128)(2,1)S(1)}, bf16[1024,1024]{1,0:T(8,128)(2,1)}, u32[]{:S(2)}) %copy-start.1) | copy-done | bytes 2097176
  5.2 1.2 %copy-done.2 = bf16[1,8,64,1024]{3,2,1,0:T(8,128)(2,1)S(1)} copy-done((bf16[1,8,64,1024]{3,2,1,0:T(8,128)(2,1)S(1)}, bf16[1,8,64,1024]{3,2,1,0:T(8,128)(2,1)}, u32[]{:S(2)}) %copy-start.2) | copy-done | bytes 1048600
  6.5 4.0 %project.1 = (bf16[16,304,128]{2,1,0:T(8,128)(2,1)S(1)}, bf16[192,1024]{1,0:T(8,128)(2,1)S(1)}) custom-call(s32[1,512]{1,0:T(1,128)S(1)} %reshape.21.mask, bf16[512,1024]{1,0:T(8,128)(2,1)S(1)} %bitcast.3, bf16[1,1024]{1,0:T(2,128)(2,1)S(1)} %reshape.23.gain, bf16[1024,2048]{1,0:T(8,128)(2,1)S(1)} %copy-done, bf16[1024,2048]{1,0:T(8,128)(2,1)S(1)} %copy-done, ...), custom_call_target="tpu_custom_call" | custom-call | tf_op jit(solution)/shard_map/project/pallas_call | solution.py:79
  10.5 0.0 copy-start.10
  10.5 0.0 copy-start.11
  10.5 0.0 copy-start.12
  10.5 39.5 %all_to_all.5.mine = bf16[16,304,128]{2,1,0:T(8,128)(2,1)S(1)} all-to-all(bf16[16,304,128]{2,1,0:T(8,128)(2,1)S(1)} %get-tuple-element.7), channel_id=1, replica_groups=mesh['win'=1,'slab'=8,'y'=2,'half'=2] {'slab','y'}, dimensions={0} | all-to-all | bytes 2490368 | tf_op jit(solution)/shard_map/all_to_all | solution.py:438
  50.0 0.0 copy-start.7
  50.0 0.0 copy-start.8
  50.0 0.0 copy-start.9
  50.0 0.1 slice.13
  50.1 0.1 collective-permute-start
  50.2 0.2 slice_reduce_fusion.1
  50.4 2.1 %collective-permute-done.other = bf16[16,208,128]{2,1,0:T(8,128)(2,1)S(1)} collective-permute-done((bf16[16,208,128]{2,1,0:T(8,128)(2,1)S(1)}, bf16[16,208,128]{2,1,0:T(8,128)(2,1)S(1)}, u32[]{:S(2)}, u32[]{:S(2)}) %collective-permute-start) | collective-permute-done | bytes 852000 | tf_op jit(solution)/shard_map/ppermute | solution.py:439
  52.5 0.2 slice_reduce_fusion
  52.7 0.1 maximum_convert_fusion.counts
  52.8 13.3 %attend.1.context = bf16[16,96,128]{2,1,0:T(8,128)(2,1)S(1)} custom-call(s32[32]{0:T(128)S(1)} %maximum_convert_fusion.counts, bf16[16,304,128]{2,1,0:T(8,128)(2,1)S(1)} %all_to_all.5.mine, bf16[16,208,128]{2,1,0:T(8,128)(2,1)S(1)} %collective-permute-done.other), custom_call_target="tpu_custom_call" | custom-call | tf_op jit(solution)/shard_map/attend/pallas_call | solution.py:152
  66.1 0.0 copy-done.3
  66.1 0.0 copy-done.4
  66.2 39.8 %finish.1 = bf16[8,64,512]{2,1,0:T(8,128)(2,1)S(1)} custom-call(bf16[16,96,128]{2,1,0:T(8,128)(2,1)S(1)} %attend.1.context, s32[1,512]{1,0:T(1,128)S(1)} %reshape.21.mask, bf16[192,1024]{1,0:T(8,128)(2,1)S(1)} %get-tuple-element.8.rows, bf16[1,1024]{1,0:T(2,128)(2,1)S(1)} %reshape.24.gain, bf16[1,512]{1,0:T(2,128)(2,1)S(1)} %reshape.25.mask_token, ...), custom_call_target="tpu_custom_call" | custom-call | tf_op jit(solution)/shard_map/finish/pallas_call | solution.py:385
  106.0 0.8 copy.18
  (18 shorter events, 0.0 us)
Async XLA Ops:
  1.4 2.2 %copy-start = (bf16[1024,2048]{1,0:T(8,128)(2,1)S(1)}, bf16[1024,2048]{1,0:T(8,128)(2,1)}, u32[]{:S(2)}) copy-start(bf16[1024,2048]{1,0:T(8,128)(2,1)} %wk.1) | copy-start | bytes 12582916
  3.6 1.6 %copy-start.1 = (bf16[1024,1024]{1,0:T(8,128)(2,1)S(1)}, bf16[1024,1024]{1,0:T(8,128)(2,1)}, u32[]{:S(2)}) copy-start(bf16[1024,1024]{1,0:T(8,128)(2,1)} %wv.1) | copy-start | bytes 6291460
  5.2 1.2 %copy-start.2 = (bf16[1,8,64,1024]{3,2,1,0:T(8,128)(2,1)S(1)}, bf16[1,8,64,1024]{3,2,1,0:T(8,128)(2,1)}, u32[]{:S(2)}) copy-start(bf16[1,8,64,1024]{3,2,1,0:T(8,128)(2,1)} %param.16) | copy-start | bytes 3145732
  10.5 39.7 %copy-start.10 = (bf16[1024]{0:T(1024)(128)(2,1)S(1)}, bf16[1024]{0:T(1024)(128)(2,1)}, u32[]{:S(2)}) copy-start(bf16[1024]{0:T(1024)(128)(2,1)} %param.22) | copy-start | bytes 6148
  10.5 39.7 %copy-start.11 = (bf16[512]{0:T(512)(128)(2,1)S(1)}, bf16[512]{0:T(512)(128)(2,1)}, u32[]{:S(2)}) copy-start(bf16[512]{0:T(512)(128)(2,1)} %param.24) | copy-start | bytes 3076
  10.5 39.7 %copy-start.12 = (bf16[512]{0:T(512)(128)(2,1)S(1)}, bf16[512]{0:T(512)(128)(2,1)}, u32[]{:S(2)}) copy-start(bf16[512]{0:T(512)(128)(2,1)} %param.28) | copy-start | bytes 3076
  50.0 16.1 %copy-start.3 = (bf16[1024,512]{1,0:T(8,128)(2,1)S(1)}, bf16[1024,512]{1,0:T(8,128)(2,1)}, u32[]{:S(2)}) copy-start(bf16[1024,512]{1,0:T(8,128)(2,1)} %embed_hbm.1) | copy-start | bytes 3145732
  50.0 16.1 %copy-start.4 = (bf16[512,1024]{1,0:T(8,128)(2,1)S(1)}, bf16[512,1024]{1,0:T(8,128)(2,1)}, u32[]{:S(2)}) copy-start(bf16[512,1024]{1,0:T(8,128)(2,1)} %wqk_hbm.1) | copy-start | bytes 3145732
  50.0 16.1 %copy-start.5 = (bf16[512,512]{1,0:T(8,128)(2,1)S(1)}, bf16[512,512]{1,0:T(8,128)(2,1)}, u32[]{:S(2)}) copy-start(bf16[512,512]{1,0:T(8,128)(2,1)} %wv_hbm.1) | copy-start | bytes 1572868
  50.0 16.1 %copy-start.6 = (bf16[512,512]{1,0:T(8,128)(2,1)S(1)}, bf16[512,512]{1,0:T(8,128)(2,1)}, u32[]{:S(2)}) copy-start(bf16[512,512]{1,0:T(8,128)(2,1)} %dec_wo_hbm.1) | copy-start | bytes 1572868
  50.0 16.1 %copy-start.7 = (bf16[64,512]{1,0:T(8,128)(2,1)S(1)}, bf16[64,512]{1,0:T(8,128)(2,1)}, u32[]{:S(2)}) copy-start(bf16[64,512]{1,0:T(8,128)(2,1)} %col_pos.1) | copy-start | bytes 196612
  50.0 16.1 %copy-start.8 = (bf16[32,512]{1,0:T(8,128)(2,1)S(1)}, bf16[32,512]{1,0:T(8,128)(2,1)}, u32[]{:S(2)}) copy-start(bf16[32,512]{1,0:T(8,128)(2,1)} %row_pos.1) | copy-start | bytes 98308
  50.0 16.1 %copy-start.9 = (bf16[8,512]{1,0:T(8,128)(2,1)S(1)}, bf16[8,512]{1,0:T(8,128)(2,1)}, u32[]{:S(2)}) copy-start(bf16[8,512]{1,0:T(8,128)(2,1)} %depth_pos.1) | copy-start | bytes 24580
  50.1 2.4 %collective-permute-start = (bf16[16,208,128]{2,1,0:T(8,128)(2,1)S(1)}, bf16[16,208,128]{2,1,0:T(8,128)(2,1)S(1)}, u32[]{:S(2)}, u32[]{:S(2)}) collective-permute-start(bf16[16,208,128]{2,1,0:T(8,128)(2,1)S(1)} %slice.13), channel_id=1, source_target_pairs={{0,1},{1,0},{2,3},{3,2},{4,5},{5,4},{6,7},{7,6},{8,9},{9,8},{10,11... | collective-permute-start | bytes 2555912 | tf_op jit(solution)/shard_map/ppermute | solution.py:439

commit v3 on v2

--- a/solution.py
+++ b/solution.py
@@ -41,64 +41,191 @@
     return lax.broadcasted_iota(jnp.int32, shape, dim)
 
 
-def project_kernel(mask, volume, gain, wq, wk, wv, sent, rows, normed):
-    tokens = volume.shape[0]
-
-    @pl.when(pl.program_id(0) == 0)
-    def _():
-        seen = mask[...] == 1
-        seen_rows = jnp.broadcast_to(jnp.where(seen, 1.0, 0.0), (16, tokens)).astype(BF16)
-        upper = jnp.where(iota((tokens, tokens), 0) <= iota((tokens, tokens), 1), 1.0, 0.0)
-        rank = dot(seen_rows, upper.astype(BF16))[0:1, :].astype(jnp.int32) - 1
-        rank = jnp.where(seen, rank, -1)
-        pick = jnp.where(iota((MOST, tokens), 0) == rank, 1.0, 0.0).astype(BF16)
-        row_data = dot(pick, volume[...])
-        rows[...] = row_data.astype(BF16)
-        normed[...] = norm(row_data, gain[...]).astype(BF16)
-
-    count = jnp.sum(jnp.where(mask[...] == 1, 1.0, 0.0), axis=1, keepdims=True)
-    x = normed[...]
-    size = wq.shape[1] // QUAD
-    q = dot(x, wq[...]) * (size ** (-0.5) * LOG2E)
-    k = dot(x, wk[...])
-    v = dot(x, wv[...])
-    for i in range(QUAD):
-        part = slice(i * size, (i + 1) * size)
-        sent[i, 0:MOST, :] = jnp.concatenate([k[:, part], v[:, part]], axis=1).astype(BF16)
-        sent[i, MOST:KV_ROWS, :] = jnp.broadcast_to(count, (COUNT_ROWS, 2 * size)).astype(BF16)
-        sent[i, KV_ROWS:SEND_ROWS, :] = jnp.concatenate(
-            [q[0:HALF, part], q[HALF:MOST, part]], axis=1
-        ).astype(BF16)
-
-
-def project(mask, volume, gain, wqk, wv):
+def mask_row(mask):
+    return jnp.concatenate([mask[0, r : r + 1, :] for r in range(mask.shape[1])], axis=1)
+
+
+def project_kernel(
+    mask,
+    gain,
+    volume_hbm,
+    wqk_hbm,
+    wv_hbm,
+    rows,
+    mine,
+    other,
+    volume,
+    wq,
+    wk,
+    wv,
+    sent,
+    load_sem,
+    send_sem,
+    recv_sem,
+    pass_send,
+    pass_recv,
+):
+    slab, y, side = lax.axis_index("slab"), lax.axis_index("y"), lax.axis_index("half")
+    y_count = lax.axis_size("y")
     tokens, width = volume.shape
-    steps = HEADS // QUAD
-    cols = width // steps
+    quads, _, cols = wq.shape
+    head = slab * y_count + y
+    own_quad = head // QUAD
+    order = [(t + 1) % quads for t in range(quads)]
+
+    first = pltpu.make_async_copy(volume_hbm, volume, load_sem.at[3 * quads])
+    first.start()
+    loads = []
+    for t in range(quads):
+        quad = lax.rem(own_quad + order[t], quads)
+        at = pl.multiple_of(quad * cols, cols)
+        group = [
+            pltpu.make_async_copy(
+                wqk_hbm.at[:, pl.ds(at, cols)], wq.at[t], load_sem.at[3 * t]
+            ),
+            pltpu.make_async_copy(
+                wqk_hbm.at[:, pl.ds(at + width, cols)], wk.at[t], load_sem.at[3 * t + 1]
+            ),
+            pltpu.make_async_copy(
+                wv_hbm.at[:, pl.ds(at, cols)], wv.at[t], load_sem.at[3 * t + 2]
+            ),
+        ]
+        for load in group:
+            load.start()
+        loads.append(group)
+
+    def place(peer):
+        return {"slab": peer // y_count, "y": lax.rem(peer, y_count)}
+
+    barrier = pltpu.get_barrier_semaphore()
+    for i in range(1, HEADS):
+        peer = lax.rem(head + i, HEADS)
+        pl.semaphore_signal(barrier, inc=1, device_id=place(peer), device_id_type=MESH)
+    pl.semaphore_signal(barrier, inc=1, device_id={"half": 1 - side}, device_id_type=MESH)
+
+    seen = mask_row(mask) == 1
+    count = jnp.sum(jnp.where(seen, 1.0, 0.0), axis=1, keepdims=True)
+    seen_rows = jnp.broadcast_to(jnp.where(seen, 1.0, 0.0), (16, tokens)).astype(BF16)
+    upper = jnp.where(iota((tokens, tokens), 0) <= iota((tokens, tokens), 1), 1.0, 0.0)
+    rank = dot(seen_rows, upper.astype(BF16))[0:1, :].astype(jnp.int32) - 1
+    rank = jnp.where(seen, rank, -1)
+    pick = jnp.where(iota((MOST, tokens), 0) == rank, 1.0, 0.0).astype(BF16)
+    first.wait()
+    row_data = dot(pick, volume[...])
+    rows[...] = row_data.astype(BF16)
+    x = norm(row_data, gain[...].astype(F32).reshape(1, width)).astype(BF16)
+    size = cols // QUAD
+    counts = jnp.broadcast_to(count, (COUNT_ROWS, 2 * size)).astype(BF16)
+    pl.semaphore_wait(barrier, HEADS)
+
+    def send(peer):
+        return pltpu.make_async_remote_copy(
+            src_ref=sent.at[peer],
+            dst_ref=mine.at[head],
+            send_sem=send_sem.at[peer],
+            recv_sem=recv_sem.at[head],
+            device_id=place(peer),
+            device_id_type=MESH,
+        )
+
+    def arrival(peer):
+        return pltpu.make_async_remote_copy(
+            src_ref=sent.at[peer],
+            dst_ref=mine.at[peer],
+            send_sem=send_sem.at[peer],
+            recv_sem=recv_sem.at[peer],
+            device_id=place(peer),
+            device_id_type=MESH,
+        )
+
+    def hand_over(peer):
+        return pltpu.make_async_remote_copy(
+            src_ref=mine.at[peer, pl.ds(0, KV_ROWS)],
+            dst_ref=other.at[peer],
+            send_sem=pass_send.at[peer],
+            recv_sem=pass_recv.at[peer],
+            device_id={"half": 1 - side},
+            device_id_type=MESH,
+        )
+
+    for t in range(quads):
+        for load in loads[t]:
+            load.wait()
+        quad = lax.rem(own_quad + order[t], quads)
+        q = dot(x, wq[t]) * (size ** (-0.5) * LOG2E)
+        k = dot(x, wk[t])
+        v = dot(x, wv[t])
+        for i in range(QUAD):
+            part = slice(i * size, (i + 1) * size)
+            peer = quad * QUAD + i
+            sent[peer, 0:MOST, :] = jnp.concatenate([k[:, part], v[:, part]], axis=1).astype(BF16)
+            sent[peer, MOST:KV_ROWS, :] = counts
+            sent[peer, KV_ROWS:SEND_ROWS, :] = jnp.concatenate(
+                [q[0:HALF, part], q[HALF:MOST, part]], axis=1
+            ).astype(BF16)
+            if order[t] > 0:
+                send(peer).start()
+            else:
+
+                @pl.when(peer != head)
+                def _():
+                    send(peer).start()
+
+    mine[head] = sent[head]
+    hand_over(head).start()
+    for t in range(quads):
+        quad = lax.rem(own_quad - order[t] + quads, quads)
+        for i in range(QUAD):
+            peer = quad * QUAD + i
+            if order[t] > 0:
+                arrival(peer).wait_recv()
+                hand_over(peer).start()
+            else:
+
+                @pl.when(peer != head)
+                def _():
+                    arrival(peer).wait_recv()
+                    hand_over(peer).start()
+
+    for i in range(1, HEADS):
+        send(lax.rem(head + i, HEADS)).wait_send()
+    for i in range(HEADS):
+        hand_over(i).wait()
+
+
+def project(mask, gain, volume, wqk, wv):
+    tokens, width = volume.shape
+    quads = HEADS // QUAD
+    cols = width // quads
     lanes = 2 * (width // HEADS)
+    whole = pl.BlockSpec(memory_space=pltpu.VMEM)
+    dma = pltpu.SemaphoreType.DMA
     return pl.pallas_call(
         project_kernel,
-        grid=(steps,),
-        in_specs=[
-            pl.BlockSpec((1, tokens), lambda j: (0, 0)),
-            pl.BlockSpec((tokens, width), lambda j: (0, 0)),
-            pl.BlockSpec((1, width), lambda j: (0, 0)),
-            pl.BlockSpec((width, cols), lambda j: (0, j)),
-            pl.BlockSpec((width, cols), lambda j: (0, j + steps)),
-            pl.BlockSpec((width, cols), lambda j: (0, j)),
+        in_specs=[whole] * 2 + [pl.BlockSpec(memory_space=pl.ANY)] * 3,
+        out_specs=[whole] * 3,
+        out_shape=[
+            jax.ShapeDtypeStruct((MOST, width), BF16),
+            jax.ShapeDtypeStruct((HEADS, SEND_ROWS, lanes), BF16),
+            jax.ShapeDtypeStruct((HEADS, KV_ROWS, lanes), BF16),
         ],
-        out_specs=[
-            pl.BlockSpec((QUAD, SEND_ROWS, lanes), lambda j: (j, 0, 0)),
-            pl.BlockSpec((MOST, width), lambda j: (0, 0)),
+        scratch_shapes=[
+            pltpu.VMEM((tokens, width), BF16),
+            pltpu.VMEM((quads, width, cols), BF16),
+            pltpu.VMEM((quads, width, cols), BF16),
+            pltpu.VMEM((quads, width, cols), BF16),
+            pltpu.VMEM((HEADS, SEND_ROWS, lanes), BF16),
+            dma((3 * quads + 1,)),
+            dma((HEADS,)),
+            dma((HEADS,)),
+            dma((HEADS,)),
+            dma((HEADS,)),
         ],
-        out_shape=[
-            jax.ShapeDtypeStruct((HEADS, SEND_ROWS, lanes), BF16),
-            jax.ShapeDtypeStruct((MOST, width), BF16),
-        ],
-        scratch_shapes=[pltpu.VMEM((MOST, width), BF16)],
-        compiler_params=pltpu.CompilerParams(vmem_limit_bytes=40 << 20),
+        compiler_params=pltpu.CompilerParams(
+            vmem_limit_bytes=52 << 20, collective_id=0, has_side_effects=True
+        ),
         name="project",
-    )(mask, volume, gain, wqk, wqk, wv)
+    )(mask, gain, volume, wqk, wv)
 
 
 TILE = 256
@@ -253,7 +380,8 @@
         head_copies.append(copy)
     landed[head] = context[head]
 
-    seen = jnp.broadcast_to(jnp.where(mask[...] == 1, 1.0, 0.0), (16, tokens)).astype(BF16)
+    seen = jnp.where(mask_row(mask) == 1, 1.0, 0.0)
+    seen = jnp.broadcast_to(seen, (16, tokens)).astype(BF16)
     down, across = iota((tokens, tokens), 0), iota((tokens, tokens), 1)
     rank = dot_nt(jnp.where(across <= down, 1.0, 0.0).astype(BF16), seen)[:, 0:1]
     shown = dot_nt(jnp.where(across == down, 1.0, 0.0).astype(BF16), seen)[:, 0:1] > 0.5
@@ -375,7 +503,7 @@
 
 
 def finish(plane_rows, depth, context, mask, rows, *others):
-    tokens = mask.shape[1]
+    tokens = mask.shape[1] * mask.shape[2]
     weights = others[-5:]
     dec_width = weights[1].shape[1]
     heads = context.shape[0]
@@ -431,12 +559,9 @@
 ):
     _, plane_rows, plane_cols, width = volume.shape
     tokens = plane_rows * plane_cols
-    mask = vis_mask.reshape(1, tokens)
-    sent, rows = project(
-        mask, volume.reshape(tokens, width), enc_gain.reshape(1, width), enc_wqk, enc_wv
+    rows, mine, other = project(
+        vis_mask, enc_gain, volume.reshape(tokens, width), enc_wqk, enc_wv
     )
-    mine = lax.all_to_all(sent, ("slab", "y"), split_axis=0, concat_axis=0, tiled=True)
-    other = lax.ppermute(mine[:, :KV_ROWS, :], "half", [(0, 1), (1, 0)])
     counts = jnp.concatenate([mine[:, MOST, 0], other[:, MOST, 0]]).astype(jnp.int32)
     window_tokens = WIN_SLABS * tokens * lax.axis_size("y") * lax.axis_size("half")
     context = attend(counts, mine, other, window_tokens // 4)
@@ -444,7 +569,7 @@
         plane_rows,
         depth_pos.shape[0],
         context,
-        mask,
+        vis_mask,
         rows,
         final_gain.reshape(1, width),
         mask_token.reshape(1, -1),

time: 108 us -> 100 us (0.926)
  blocking collectives: 39.5 us -> 0 us
  Pallas kernels: 57.1 us -> 94.1 us
  local copies, waits for them, and re-layouts: 7.78 us -> 4.51 us
  waiting for transfers between devices: 2.09 us -> 0 us
    all_to_all x1 -> x0, blocking collectives: 39.5 us -> none  [per_device(): lax.all_to_all(sent, ('slab', 'y'), split_axis=0, concat_axis=0, tiled=True)]
    pallas_call x1, Pallas kernels: 4 us -> 29.5 us  [project(): pl.pallas_call(project_kernel, in_specs=[whole] * 2 + [pl.BlockSpec(memor...]
    pallas_call x1, Pallas kernels: 39.8 us -> 51.3 us  [finish(): pl.pallas_call(functools.partial(finish_kernel, plane_rows), in_specs=[wh...]
    unnamed x27 -> x29, local copies, waits for them, and re-layouts: 5.85 us -> 3.51 us
    ppermute x1 -> x0, waiting for transfers between devices: 2.09 us -> none  [per_device(): other = lax.ppermute(mine[:, :KV_ROWS, :], 'half', [(0, 1), (1, 0)])]
    reshape x2 -> x0, local copies, waits for them, and re-layouts: 1.45 us -> none  [the longest x1 0.76 us: per_device(): mask = vis_mask.reshape(1, tokens)]
  transfers between devices with their start and end apart: 1 -> 0, of which waited for: 1 -> 0; matrix products, arithmetic and copies ran while one was open for 0% -> 0% of each run, Pallas kernels for 0% -> 0%
where the time goes in v3:
time: 100 us; the launch traced here: 98.8 us
  Pallas kernels  94.1 us (94%)
  local copies, waits for them, and re-layouts  4.51 us (5%)
    pallas_call x1, Pallas kernels, finish(): pl.pallas_call(functools.partial(finish_kernel, plane_rows), in_specs=[wh...  51.3 us
    pallas_call x1, Pallas kernels, project(): pl.pallas_call(project_kernel, in_specs=[whole] * 2 + [pl.BlockSpec(memor...  29.5 us
    pallas_call x1, Pallas kernels, attend(): pl.pallas_call(attend_kernel, in_specs=[pl.BlockSpec(memory_space=pltpu.S...  13.3 us
    unnamed x29, local copies, waits for them, and re-layouts  3.51 us

profile of v3, /device:TPU:0, one launch (start us, length us, event | category | flops | bytes accessed | tf_op | source)
XLA Modules:
  0.0 98.8 jit_solution(1998897419512386956)
XLA Ops:
  0.0 0.7 copy-done.7
  0.7 0.7 copy-done.10
  1.4 0.0 copy-start.5
  1.4 0.0 copy-start.6
  1.4 29.5 %project.1 = (bf16[192,1024]{1,0:T(8,128)(2,1)S(1)}, bf16[16,304,128]{2,1,0:T(8,128)(2,1)}, bf16[16,208,128]{2,1,0:T(8,128)(2,1)S(1)}) custom-call(s32[1,8,64]{2,1,0:T(8,128)S(1)} %copy-done.7, bf16[1024]{0:T(1024)(128)(2,1)S(1)} %copy-done.10, bf16[512,1024]{1,0:T(8,128)(2,1)} %bitcast.3, bf16[1024,2048]{1,0:T(8,128)(2,1)} %wqk_hbm.2, bf16[1024,1024]{1,0:T(8,128)(2,1)} %wv_hbm.2), custom_call_target="tpu_custom_call" | custom-call | tf_op jit(solution)/shard_map/project/pallas_call | solution.py:203
  30.9 0.0 copy-start.11
  30.9 0.0 copy-start.12
  30.9 0.0 copy-start.13
  31.0 0.0 copy-start.8
  31.0 0.0 copy-start.9
  31.0 1.0 slice_reduce_fusion
  32.0 0.1 maximum_convert_fusion.counts
  32.1 1.3 %copy-done = bf16[16,304,128]{2,1,0:T(8,128)(2,1)S(1)} copy-done((bf16[16,304,128]{2,1,0:T(8,128)(2,1)S(1)}, bf16[16,304,128]{2,1,0:T(8,128)(2,1)}, u32[]{:S(2)}) %copy-start) | copy-done | bytes 1245208
  33.3 13.3 %attend.1.context = bf16[16,96,128]{2,1,0:T(8,128)(2,1)S(1)} custom-call(s32[32]{0:T(128)S(1)} %maximum_convert_fusion.counts, bf16[16,304,128]{2,1,0:T(8,128)(2,1)S(1)} %copy-done, bf16[16,208,128]{2,1,0:T(8,128)(2,1)S(1)} %get-tuple-element.9.other), custom_call_target="tpu_custom_call" | custom-call | tf_op jit(solution)/shard_map/attend/pallas_call | solution.py:279
  46.6 0.0 copy-done.11
  46.6 0.0 copy-done.12
  46.6 0.0 copy-done.13
  46.7 0.0 copy-done.1
  46.7 0.0 copy-done.2
  46.7 0.0 copy-done.3
  46.7 0.0 copy-done.4
  46.7 0.0 copy-done.5
  46.8 51.3 %finish.1 = bf16[8,64,512]{2,1,0:T(8,128)(2,1)S(1)} custom-call(bf16[16,96,128]{2,1,0:T(8,128)(2,1)S(1)} %attend.1.context, s32[1,8,64]{2,1,0:T(8,128)S(1)} %copy-done.8, bf16[192,1024]{1,0:T(8,128)(2,1)S(1)} %get-tuple-element.10.rows, bf16[1,1024]{1,0:T(2,128)(2,1)S(1)} %reshape.16.gain, bf16[1,512]{1,0:T(2,128)(2,1)S(1)} %reshape.17.mask_token, ...), custom_call_target="tpu_custom_call" | custom-call | tf_op jit(solution)/shard_map/finish/pallas_call | solution.py:513
  98.0 0.8 copy.18
  (13 shorter events, 0.0 us)
Async XLA Ops:
  0.0 0.7 copy-start.7
  0.7 0.7 copy-start.10
  1.4 45.3 %copy-start.1 = (bf16[1024,512]{1,0:T(8,128)(2,1)S(1)}, bf16[1024,512]{1,0:T(8,128)(2,1)}, u32[]{:S(2)}) copy-start(bf16[1024,512]{1,0:T(8,128)(2,1)} %embed_hbm.1) | copy-start | bytes 3145732
  1.4 45.3 %copy-start.2 = (bf16[512,1024]{1,0:T(8,128)(2,1)S(1)}, bf16[512,1024]{1,0:T(8,128)(2,1)}, u32[]{:S(2)}) copy-start(bf16[512,1024]{1,0:T(8,128)(2,1)} %wqk_hbm.3) | copy-start | bytes 3145732
  1.4 45.3 %copy-start.3 = (bf16[512,512]{1,0:T(8,128)(2,1)S(1)}, bf16[512,512]{1,0:T(8,128)(2,1)}, u32[]{:S(2)}) copy-start(bf16[512,512]{1,0:T(8,128)(2,1)} %wv_hbm.3) | copy-start | bytes 1572868
  1.4 45.3 %copy-start.4 = (bf16[512,512]{1,0:T(8,128)(2,1)S(1)}, bf16[512,512]{1,0:T(8,128)(2,1)}, u32[]{:S(2)}) copy-start(bf16[512,512]{1,0:T(8,128)(2,1)} %dec_wo_hbm.1) | copy-start | bytes 1572868
  1.4 45.3 %copy-start.5 = (bf16[64,512]{1,0:T(8,128)(2,1)S(1)}, bf16[64,512]{1,0:T(8,128)(2,1)}, u32[]{:S(2)}) copy-start(bf16[64,512]{1,0:T(8,128)(2,1)} %col_pos.1) | copy-start | bytes 196612
  1.4 45.3 %copy-start.6 = (bf16[32,512]{1,0:T(8,128)(2,1)S(1)}, bf16[32,512]{1,0:T(8,128)(2,1)}, u32[]{:S(2)}) copy-start(bf16[32,512]{1,0:T(8,128)(2,1)} %row_pos.1) | copy-start | bytes 98308
  30.9 15.7 %copy-start.11 = (bf16[1024]{0:T(1024)(128)(2,1)S(1)}, bf16[1024]{0:T(1024)(128)(2,1)}, u32[]{:S(2)}) copy-start(bf16[1024]{0:T(1024)(128)(2,1)} %param.22) | copy-start | bytes 6148
  30.9 15.7 %copy-start.12 = (bf16[512]{0:T(512)(128)(2,1)S(1)}, bf16[512]{0:T(512)(128)(2,1)}, u32[]{:S(2)}) copy-start(bf16[512]{0:T(512)(128)(2,1)} %param.24) | copy-start | bytes 3076
  30.9 15.7 %copy-start.13 = (bf16[512]{0:T(512)(128)(2,1)S(1)}, bf16[512]{0:T(512)(128)(2,1)}, u32[]{:S(2)}) copy-start(bf16[512]{0:T(512)(128)(2,1)} %param.28) | copy-start | bytes 3076
  31.0 15.8 %copy-start.8 = (s32[1,8,64]{2,1,0:T(8,128)S(1)}, s32[1,8,64]{2,1,0:T(8,128)}, u32[]{:S(2)}) copy-start(s32[1,8,64]{2,1,0:T(8,128)} %mask.3) | copy-start | bytes 6148
  31.0 15.8 %copy-start.9 = (bf16[8,512]{1,0:T(8,128)(2,1)S(1)}, bf16[8,512]{1,0:T(8,128)(2,1)}, u32[]{:S(2)}) copy-start(bf16[8,512]{1,0:T(8,128)(2,1)} %depth_pos.1) | copy-start | bytes 24580
  32.1 1.3 %copy-start = (bf16[16,304,128]{2,1,0:T(8,128)(2,1)S(1)}, bf16[16,304,128]{2,1,0:T(8,128)(2,1)}, u32[]{:S(2)}) copy-start(bf16[16,304,128]{2,1,0:T(8,128)(2,1)} %get-tuple-element.8.mine) | copy-start | bytes 3735556

commit v4 on v3

--- a/solution.py
+++ b/solution.py
@@ -39,6 +39,14 @@
 
 def iota(shape, dim):
     return lax.broadcasted_iota(jnp.int32, shape, dim)
+
+
+def flip(position, bits, count):
+    result, weight = 0, 1
+    while weight < count:
+        result = result + lax.rem(position // weight + bits // weight, 2) * weight
+        weight *= 2
+    return result
 
 
 def mask_row(mask):
@@ -71,13 +79,13 @@
     quads, _, cols = wq.shape
     head = slab * y_count + y
     own_quad = head // QUAD
-    order = [(t + 1) % quads for t in range(quads)]
+    order = [quads // 2 + t for t in range(quads // 2)] + list(range(quads // 2 - 1, -1, -1))
 
     first = pltpu.make_async_copy(volume_hbm, volume, load_sem.at[3 * quads])
     first.start()
     loads = []
     for t in range(quads):
-        quad = lax.rem(own_quad + order[t], quads)
+        quad = flip(own_quad, order[t], quads)
         at = pl.multiple_of(quad * cols, cols)
         group = [
             pltpu.make_async_copy(
@@ -151,7 +159,7 @@
     for t in range(quads):
         for load in loads[t]:
             load.wait()
-        quad = lax.rem(own_quad + order[t], quads)
+        quad = flip(own_quad, order[t], quads)
         q = dot(x, wq[t]) * (size ** (-0.5) * LOG2E)
         k = dot(x, wk[t])
         v = dot(x, wv[t])
@@ -174,7 +182,7 @@
     mine[head] = sent[head]
     hand_over(head).start()
     for t in range(quads):
-        quad = lax.rem(own_quad - order[t] + quads, quads)
+        quad = flip(own_quad, order[t], quads)
         for i in range(QUAD):
             peer = quad * QUAD + i
             if order[t] > 0:
@@ -349,11 +357,11 @@
         loads.append(load)
 
     def head_device(i):
-        peer = lax.rem(head + i, heads)
+        peer = flip(head, heads - i, heads)
         return peer, {"slab": peer // y_count, "y": lax.rem(peer, y_count)}
 
     def level_device(i):
-        peer = lax.rem(level + i, depth)
+        peer = flip(level, depth - i, depth)
         return peer, {"win": peer // slab_count, "slab": lax.rem(peer, slab_count)}
 
     barrier = pltpu.get_barrier_semaphore()
@@ -476,9 +484,7 @@
 
     def decode(z):
         product = (keys[...] * queries[z][None]).reshape(tokens, dec_width)
-        high = product.astype(BF16)
-        low = (product - high.astype(F32)).astype(BF16)
-        scores = (dot(high, gather) + dot(low, gather)) * dec_size ** (-0.5)
+        scores = dot(product.astype(BF16), gather) * dec_size ** (-0.5)
         scores = scores.reshape(depth, spots, wide)
         exponent = jnp.exp(scores - jnp.max(scores, axis=0, keepdims=True))
         probs = exponent / jnp.sum(exponent, axis=0, keepdims=True)
@@ -487,7 +493,7 @@
         return (columns[z].astype(F32) + dot(result, dec_wo[...])).astype(BF16)
 
     def step(i, carry):
-        z = lax.rem(level + i, depth)
+        z = flip(level, depth - i, depth)
         decoded[z] = decode(z)
         back_copy(i).start()
         return carry

time: 100 us -> 98.4 us (0.984)
  no operation moved by 1% of the time
where the time goes in v4:
time: 98.4 us; the launch traced here: 98.1 us
  Pallas kernels  93.3 us (95%)
  local copies, waits for them, and re-layouts  4.51 us (5%)
    pallas_call x1, Pallas kernels, finish(): pl.pallas_call(functools.partial(finish_kernel, plane_rows), in_specs=[wh...  50.5 us
    pallas_call x1, Pallas kernels, project(): pl.pallas_call(project_kernel, in_specs=[whole] * 2 + [pl.BlockSpec(memor...  29.5 us
    pallas_call x1, Pallas kernels, attend(): pl.pallas_call(attend_kernel, in_specs=[pl.BlockSpec(memory_space=pltpu.S...  13.3 us
    unnamed x29, local copies, waits for them, and re-layouts  3.51 us

profile of v4, /device:TPU:0, one launch (start us, length us, event | category | flops | bytes accessed | tf_op | source)
XLA Modules:
  0.0 98.1 jit_solution(8545636403973953477)
XLA Ops:
  0.0 0.7 copy-done.7
  0.7 0.7 copy-done.10
  1.4 0.0 copy-start.5
  1.4 0.0 copy-start.6
  1.4 29.5 %project.1 = (bf16[192,1024]{1,0:T(8,128)(2,1)S(1)}, bf16[16,304,128]{2,1,0:T(8,128)(2,1)}, bf16[16,208,128]{2,1,0:T(8,128)(2,1)S(1)}) custom-call(s32[1,8,64]{2,1,0:T(8,128)S(1)} %copy-done.7, bf16[1024]{0:T(1024)(128)(2,1)S(1)} %copy-done.10, bf16[512,1024]{1,0:T(8,128)(2,1)} %bitcast.3, bf16[1024,2048]{1,0:T(8,128)(2,1)} %wqk_hbm.2, bf16[1024,1024]{1,0:T(8,128)(2,1)} %wv_hbm.2), custom_call_target="tpu_custom_call" | custom-call | tf_op jit(solution)/shard_map/project/pallas_call | solution.py:211
  30.9 0.0 copy-start.11
  31.0 0.0 copy-start.12
  31.0 0.0 copy-start.13
  31.0 0.0 copy-start.8
  31.0 0.0 copy-start.9
  31.0 1.0 %slice_reduce_fusion = (bf16[16]{0:T(256)(128)(2,1)S(1)}, bf16[16]{0:T(256)(128)(2,1)S(1)}) fusion(bf16[16,208,128]{2,1,0:T(8,128)(2,1)S(1)} %get-tuple-element.9.other, bf16[16,304,128]{2,1,0:T(8,128)(2,1)} %get-tuple-element.8.mine), kind=kLoop, calls=%fused_computation | loop fusion | bytes 128 | tf_op jit(solution)/shard_map/slice | solution.py:571
  32.0 0.1 maximum_convert_fusion.counts
  32.1 1.3 %copy-done = bf16[16,304,128]{2,1,0:T(8,128)(2,1)S(1)} copy-done((bf16[16,304,128]{2,1,0:T(8,128)(2,1)S(1)}, bf16[16,304,128]{2,1,0:T(8,128)(2,1)}, u32[]{:S(2)}) %copy-start) | copy-done | bytes 1245208
  33.4 13.3 %attend.1.context = bf16[16,96,128]{2,1,0:T(8,128)(2,1)S(1)} custom-call(s32[32]{0:T(128)S(1)} %maximum_convert_fusion.counts, bf16[16,304,128]{2,1,0:T(8,128)(2,1)S(1)} %copy-done, bf16[16,208,128]{2,1,0:T(8,128)(2,1)S(1)} %get-tuple-element.9.other), custom_call_target="tpu_custom_call" | custom-call | tf_op jit(solution)/shard_map/attend/pallas_call | solution.py:287
  46.7 0.0 copy-done.13
  46.7 0.0 copy-done.1
  46.7 0.0 copy-done.2
  46.7 0.0 copy-done.3
  46.7 0.0 copy-done.4
  46.7 0.0 copy-done.5
  46.7 0.0 copy-done.6
  46.8 0.0 copy-done.8
  46.8 50.5 %finish.1 = bf16[8,64,512]{2,1,0:T(8,128)(2,1)S(1)} custom-call(bf16[16,96,128]{2,1,0:T(8,128)(2,1)S(1)} %attend.1.context, s32[1,8,64]{2,1,0:T(8,128)S(1)} %copy-done.8, bf16[192,1024]{1,0:T(8,128)(2,1)S(1)} %get-tuple-element.10.rows, bf16[1,1024]{1,0:T(2,128)(2,1)S(1)} %reshape.16.gain, bf16[1,512]{1,0:T(2,128)(2,1)S(1)} %reshape.17.mask_token, ...), custom_call_target="tpu_custom_call" | custom-call | tf_op jit(solution)/shard_map/finish/pallas_call | solution.py:519
  97.3 0.8 copy.18
  (13 shorter events, 0.0 us)
Async XLA Ops:
  0.0 0.7 copy-start.7
  0.7 0.7 copy-start.10
  1.4 45.3 %copy-start.1 = (bf16[1024,512]{1,0:T(8,128)(2,1)S(1)}, bf16[1024,512]{1,0:T(8,128)(2,1)}, u32[]{:S(2)}) copy-start(bf16[1024,512]{1,0:T(8,128)(2,1)} %embed_hbm.1) | copy-start | bytes 3145732
  1.4 45.3 %copy-start.2 = (bf16[512,1024]{1,0:T(8,128)(2,1)S(1)}, bf16[512,1024]{1,0:T(8,128)(2,1)}, u32[]{:S(2)}) copy-start(bf16[512,1024]{1,0:T(8,128)(2,1)} %wqk_hbm.3) | copy-start | bytes 3145732
  1.4 45.3 %copy-start.3 = (bf16[512,512]{1,0:T(8,128)(2,1)S(1)}, bf16[512,512]{1,0:T(8,128)(2,1)}, u32[]{:S(2)}) copy-start(bf16[512,512]{1,0:T(8,128)(2,1)} %wv_hbm.3) | copy-start | bytes 1572868
  1.4 45.4 %copy-start.4 = (bf16[512,512]{1,0:T(8,128)(2,1)S(1)}, bf16[512,512]{1,0:T(8,128)(2,1)}, u32[]{:S(2)}) copy-start(bf16[512,512]{1,0:T(8,128)(2,1)} %dec_wo_hbm.1) | copy-start | bytes 1572868
  1.4 45.4 %copy-start.5 = (bf16[64,512]{1,0:T(8,128)(2,1)S(1)}, bf16[64,512]{1,0:T(8,128)(2,1)}, u32[]{:S(2)}) copy-start(bf16[64,512]{1,0:T(8,128)(2,1)} %col_pos.1) | copy-start | bytes 196612
  1.4 45.4 %copy-start.6 = (bf16[32,512]{1,0:T(8,128)(2,1)S(1)}, bf16[32,512]{1,0:T(8,128)(2,1)}, u32[]{:S(2)}) copy-start(bf16[32,512]{1,0:T(8,128)(2,1)} %row_pos.1) | copy-start | bytes 98308
  30.9 15.7 %copy-start.11 = (bf16[1024]{0:T(1024)(128)(2,1)S(1)}, bf16[1024]{0:T(1024)(128)(2,1)}, u32[]{:S(2)}) copy-start(bf16[1024]{0:T(1024)(128)(2,1)} %param.22) | copy-start | bytes 6148
  31.0 15.7 %copy-start.12 = (bf16[512]{0:T(512)(128)(2,1)S(1)}, bf16[512]{0:T(512)(128)(2,1)}, u32[]{:S(2)}) copy-start(bf16[512]{0:T(512)(128)(2,1)} %param.24) | copy-start | bytes 3076
  31.0 15.7 %copy-start.13 = (bf16[512]{0:T(512)(128)(2,1)S(1)}, bf16[512]{0:T(512)(128)(2,1)}, u32[]{:S(2)}) copy-start(bf16[512]{0:T(512)(128)(2,1)} %param.28) | copy-start | bytes 3076
  31.0 15.8 %copy-start.8 = (s32[1,8,64]{2,1,0:T(8,128)S(1)}, s32[1,8,64]{2,1,0:T(8,128)}, u32[]{:S(2)}) copy-start(s32[1,8,64]{2,1,0:T(8,128)} %mask.3) | copy-start | bytes 6148
  31.0 15.8 %copy-start.9 = (bf16[8,512]{1,0:T(8,128)(2,1)S(1)}, bf16[8,512]{1,0:T(8,128)(2,1)}, u32[]{:S(2)}) copy-start(bf16[8,512]{1,0:T(8,128)(2,1)} %depth_pos.1) | copy-start | bytes 24580
  32.1 1.3 %copy-start = (bf16[16,304,128]{2,1,0:T(8,128)(2,1)S(1)}, bf16[16,304,128]{2,1,0:T(8,128)(2,1)}, u32[]{:S(2)}) copy-start(bf16[16,304,128]{2,1,0:T(8,128)(2,1)} %get-tuple-element.8.mine) | copy-start | bytes 3735556

commit v5 on v4

--- a/solution.py
+++ b/solution.py
@@ -275,7 +275,7 @@
         results[pl.ds(at, TILE), :] = mixed / pltpu.roll(mixed, size, 1)
         return carry
 
-    lax.fori_loop(0, half // TILE, step, 0)
+    lax.fori_loop(0, half // TILE, step, 0, unroll=2)
     for i in range(blocks):
         block = results[pl.ds(starts[i], MOST), :][:, size:]
         out[i, :, :] = jnp.concatenate([block[0:HALF], block[HALF:MOST]], axis=1).astype(BF16)

time: 98.4 us -> 97.4 us (0.990)
  no operation moved by 1% of the time
where the time goes in v5:
time: 97.4 us; the launch traced here: 97.2 us
  Pallas kernels  92.4 us (95%)
  local copies, waits for them, and re-layouts  4.51 us (5%)
    pallas_call x1, Pallas kernels, finish(): pl.pallas_call(functools.partial(finish_kernel, plane_rows), in_specs=[wh...  50.5 us
    pallas_call x1, Pallas kernels, project(): pl.pallas_call(project_kernel, in_specs=[whole] * 2 + [pl.BlockSpec(memor...  29.5 us
    pallas_call x1, Pallas kernels, attend(): pl.pallas_call(attend_kernel, in_specs=[pl.BlockSpec(memory_space=pltpu.S...  12.4 us
    unnamed x29, local copies, waits for them, and re-layouts  3.51 us

profile of v5, /device:TPU:0, one launch (start us, length us, event | category | flops | bytes accessed | tf_op | source)
XLA Modules:
  0.0 97.2 jit_solution(1342722852807616821)
XLA Ops:
  0.0 0.7 copy-done.7
  0.7 0.7 copy-done.10
  1.4 29.5 %project.1 = (bf16[192,1024]{1,0:T(8,128)(2,1)S(1)}, bf16[16,304,128]{2,1,0:T(8,128)(2,1)}, bf16[16,208,128]{2,1,0:T(8,128)(2,1)S(1)}) custom-call(s32[1,8,64]{2,1,0:T(8,128)S(1)} %copy-done.7, bf16[1024]{0:T(1024)(128)(2,1)S(1)} %copy-done.10, bf16[512,1024]{1,0:T(8,128)(2,1)} %bitcast.3, bf16[1024,2048]{1,0:T(8,128)(2,1)} %wqk_hbm.2, bf16[1024,1024]{1,0:T(8,128)(2,1)} %wv_hbm.2), custom_call_target="tpu_custom_call" | custom-call | tf_op jit(solution)/shard_map/project/pallas_call | solution.py:211
  30.9 0.0 copy-start.11
  31.0 0.0 copy-start.12
  31.0 0.0 copy-start.13
  31.0 0.0 copy-start.8
  31.0 0.0 copy-start.9
  31.0 1.0 %slice_reduce_fusion = (bf16[16]{0:T(256)(128)(2,1)S(1)}, bf16[16]{0:T(256)(128)(2,1)S(1)}) fusion(bf16[16,208,128]{2,1,0:T(8,128)(2,1)S(1)} %get-tuple-element.9.other, bf16[16,304,128]{2,1,0:T(8,128)(2,1)} %get-tuple-element.8.mine), kind=kLoop, calls=%fused_computation | loop fusion | bytes 128 | tf_op jit(solution)/shard_map/slice | solution.py:571
  32.0 0.1 maximum_convert_fusion.counts
  32.1 1.3 %copy-done = bf16[16,304,128]{2,1,0:T(8,128)(2,1)S(1)} copy-done((bf16[16,304,128]{2,1,0:T(8,128)(2,1)S(1)}, bf16[16,304,128]{2,1,0:T(8,128)(2,1)}, u32[]{:S(2)}) %copy-start) | copy-done | bytes 1245208
  33.4 12.4 %attend.1.context = bf16[16,96,128]{2,1,0:T(8,128)(2,1)S(1)} custom-call(s32[32]{0:T(128)S(1)} %maximum_convert_fusion.counts, bf16[16,304,128]{2,1,0:T(8,128)(2,1)S(1)} %copy-done, bf16[16,208,128]{2,1,0:T(8,128)(2,1)S(1)} %get-tuple-element.9.other), custom_call_target="tpu_custom_call" | custom-call | tf_op jit(solution)/shard_map/attend/pallas_call | solution.py:287
  45.8 0.0 copy-done.12
  45.8 0.0 copy-done.13
  45.8 0.0 copy-done.1
  45.8 0.0 copy-done.2
  45.8 0.0 copy-done.3
  45.8 0.0 copy-done.4
  45.8 0.0 copy-done.5
  45.9 0.0 copy-done.6
  45.9 0.0 copy-done.8
  45.9 0.0 copy-done.9
  45.9 50.5 %finish.1 = bf16[8,64,512]{2,1,0:T(8,128)(2,1)S(1)} custom-call(bf16[16,96,128]{2,1,0:T(8,128)(2,1)S(1)} %attend.1.context, s32[1,8,64]{2,1,0:T(8,128)S(1)} %copy-done.8, bf16[192,1024]{1,0:T(8,128)(2,1)S(1)} %get-tuple-element.10.rows, bf16[1,1024]{1,0:T(2,128)(2,1)S(1)} %reshape.16.gain, bf16[1,512]{1,0:T(2,128)(2,1)S(1)} %reshape.17.mask_token, ...), custom_call_target="tpu_custom_call" | custom-call | tf_op jit(solution)/shard_map/finish/pallas_call | solution.py:519
  96.4 0.8 copy.18
  (13 shorter events, 0.0 us)
Async XLA Ops:
  0.0 0.7 copy-start.7
  0.7 0.7 copy-start.10
  1.4 44.4 %copy-start.1 = (bf16[1024,512]{1,0:T(8,128)(2,1)S(1)}, bf16[1024,512]{1,0:T(8,128)(2,1)}, u32[]{:S(2)}) copy-start(bf16[1024,512]{1,0:T(8,128)(2,1)} %embed_hbm.1) | copy-start | bytes 3145732
  1.4 44.4 %copy-start.2 = (bf16[512,1024]{1,0:T(8,128)(2,1)S(1)}, bf16[512,1024]{1,0:T(8,128)(2,1)}, u32[]{:S(2)}) copy-start(bf16[512,1024]{1,0:T(8,128)(2,1)} %wqk_hbm.3) | copy-start | bytes 3145732
  1.4 44.5 %copy-start.3 = (bf16[512,512]{1,0:T(8,128)(2,1)S(1)}, bf16[512,512]{1,0:T(8,128)(2,1)}, u32[]{:S(2)}) copy-start(bf16[512,512]{1,0:T(8,128)(2,1)} %wv_hbm.3) | copy-start | bytes 1572868
  1.4 44.5 %copy-start.4 = (bf16[512,512]{1,0:T(8,128)(2,1)S(1)}, bf16[512,512]{1,0:T(8,128)(2,1)}, u32[]{:S(2)}) copy-start(bf16[512,512]{1,0:T(8,128)(2,1)} %dec_wo_hbm.1) | copy-start | bytes 1572868
  1.4 44.5 %copy-start.5 = (bf16[64,512]{1,0:T(8,128)(2,1)S(1)}, bf16[64,512]{1,0:T(8,128)(2,1)}, u32[]{:S(2)}) copy-start(bf16[64,512]{1,0:T(8,128)(2,1)} %col_pos.1) | copy-start | bytes 196612
  1.4 44.5 %copy-start.6 = (bf16[32,512]{1,0:T(8,128)(2,1)S(1)}, bf16[32,512]{1,0:T(8,128)(2,1)}, u32[]{:S(2)}) copy-start(bf16[32,512]{1,0:T(8,128)(2,1)} %row_pos.1) | copy-start | bytes 98308
  30.9 14.8 %copy-start.11 = (bf16[1024]{0:T(1024)(128)(2,1)S(1)}, bf16[1024]{0:T(1024)(128)(2,1)}, u32[]{:S(2)}) copy-start(bf16[1024]{0:T(1024)(128)(2,1)} %param.22) | copy-start | bytes 6148
  31.0 14.8 %copy-start.12 = (bf16[512]{0:T(512)(128)(2,1)S(1)}, bf16[512]{0:T(512)(128)(2,1)}, u32[]{:S(2)}) copy-start(bf16[512]{0:T(512)(128)(2,1)} %param.24) | copy-start | bytes 3076
  31.0 14.8 %copy-start.13 = (bf16[512]{0:T(512)(128)(2,1)S(1)}, bf16[512]{0:T(512)(128)(2,1)}, u32[]{:S(2)}) copy-start(bf16[512]{0:T(512)(128)(2,1)} %param.28) | copy-start | bytes 3076
  31.0 14.9 %copy-start.8 = (s32[1,8,64]{2,1,0:T(8,128)S(1)}, s32[1,8,64]{2,1,0:T(8,128)}, u32[]{:S(2)}) copy-start(s32[1,8,64]{2,1,0:T(8,128)} %mask.3) | copy-start | bytes 6148
  31.0 14.9 %copy-start.9 = (bf16[8,512]{1,0:T(8,128)(2,1)S(1)}, bf16[8,512]{1,0:T(8,128)(2,1)}, u32[]{:S(2)}) copy-start(bf16[8,512]{1,0:T(8,128)(2,1)} %depth_pos.1) | copy-start | bytes 24580
  32.1 1.3 %copy-start = (bf16[16,304,128]{2,1,0:T(8,128)(2,1)S(1)}, bf16[16,304,128]{2,1,0:T(8,128)(2,1)}, u32[]{:S(2)}) copy-start(bf16[16,304,128]{2,1,0:T(8,128)(2,1)} %get-tuple-element.8.mine) | copy-start | bytes 3735556
